TPU v7x, 256 devices: a whole 4x4x8 slice. The times are simulated.
256 devices in a mesh: section: 16 (over y, z_lo), tensor: 8 (over x, core), group: 2 (over z_hi).
Axes of the slice: x: 4, y: 4, z: 8 (z_hi: 2, z_lo: 4; z = z_hi * 4 + z_lo), core: 2. Of those that a mesh axis runs over, the one named last changes fastest.
Arguments:
- ref_input: bfloat16 [2, 2, 128, 16384], P('group', None, None, 'tensor'), may hold values from -40 to 40
- norm_gain: float32 [16, 16384], P('section', 'tensor'), may hold values from 0.1 to 1.9
- w_in: bfloat16 [16, 16384, 768], P('section', 'tensor'), may hold values from -0.046875 to 0.046875
- w_out: bfloat16 [16, 384, 16384], P('section', None, 'tensor'), may hold values from -0.3125 to 0.3125
- policy_hidden: bfloat16 [512, 16384], P('group', 'tensor'), may hold values from -40 to 40
- heads: bfloat16 [2, 16384, 16384], P('group', 'section', 'tensor'), may hold values from -1 to 1
- sampled: int32 [512], replicated, may hold values from 0 to 16383
- live_mask: int32 [512], replicated, may hold values 0 or 1
- rewards: float32 [8], replicated, may hold values from -8 to 8
- prompt_ids: int32 [8], replicated, may hold values from 0 to 1, as said below
Outputs:
- token_kl: float32 [512], P(('tensor', 'group'))
- token_loss: float32 [512], P(('tensor', 'group'))
Inputs may be any that keep to these rules, and one draw needn't show every extreme that they name: `prompt_ids`: each of the 2 prompts is answered by exactly 4 responses.
All inputs are finite; a program needn't handle non-finite values.
Results may differ from a plain program's by a relative error of at most 0.017.
Values may be sent and summed in bfloat16 or wider, within the bound.
A program may use at most 64 MiB of HBM per device.

v0:
```python
import jax
import jax.numpy as jnp
from jax import lax
from jax.sharding import PartitionSpec as P

RLEN = 64


epsilon = 1e-05
penalty = 0.04


def from_behind(value, axis, steps):
    count = lax.axis_size(axis)
    pairs = [(source, (source + steps) % count) for source in range(count)]
    return lax.ppermute(value, axis, pairs)


def spread_2(x, axis, root):
    mine = lax.axis_index(axis) == root
    return lax.psum(jnp.where(mine, x, jnp.zeros_like(x)), axis)


def from_partner(block, axis, apart):
    count = lax.axis_size(axis)
    route = []
    for low in range(count):
        high = low | 1 << apart
        if high != low and high < count:
            route += [(low, high), (high, low)]
    return lax.ppermute(block, axis, route)


def advantages(rewards, prompt_ids):
    same = (prompt_ids[:, None] == prompt_ids[None, :]).astype(jnp.float32)
    counts = jnp.sum(same, axis=1)
    means = jnp.sum(same * rewards[None, :], axis=1) / counts
    spread = rewards[None, :] - means[:, None]
    variance = jnp.sum(same * spread * spread, axis=1) / counts
    return (rewards - means) / jnp.maximum(jnp.sqrt(variance), 1.0)


def shards(
    ref_input, norm_gain, w_in, w_out, policy_hidden, heads, sampled, live_mask, rewards, prompt_ids
):
    tensor_count = lax.axis_size("tensor")
    section_count = lax.axis_size("section")
    section_here = lax.axis_index("section")
    inputs = ref_input[0]
    batches = inputs.shape[0]
    row_count = inputs.shape[1]
    width = inputs.shape[2]
    full_width = width * tensor_count
    gain_row = norm_gain[0]
    weight_in = w_in[0]
    weight_out = w_out[0]
    units = weight_out.shape[0]

    def apply_layer(stream):
        values = stream.astype(jnp.float32)
        squares = lax.psum(jnp.sum(values * values, axis=1), "tensor") / full_width
        normed = (values * lax.rsqrt(squares + epsilon)[:, None] * gain_row[None, :]).astype(
            jnp.bfloat16
        )
        mixed = jnp.dot(normed, weight_in, preferred_element_type=jnp.float32)
        summed = lax.psum(mixed, "tensor")
        hidden = (jax.nn.silu(summed[:, :units]) * summed[:, units:]).astype(jnp.bfloat16)
        update = jnp.dot(hidden, weight_out, preferred_element_type=jnp.float32)
        return (values + update).astype(jnp.bfloat16)

    def relay_step(step_index, carry):
        incoming, finished = carry
        fresh = lax.dynamic_index_in_dim(
            inputs, jnp.minimum(step_index, batches - 1), 0, keepdims=False
        )
        entering = jnp.logical_and(section_here == 0, step_index < batches)
        stream = jnp.where(entering, fresh, incoming)
        arrived = from_behind(apply_layer(stream), "section", 1)
        slot_index = step_index - (section_count - 1)
        placed = lax.dynamic_update_index_in_dim(
            finished, arrived, jnp.clip(slot_index, 0, batches - 1), 0
        )
        storing = jnp.logical_and(section_here == 0, slot_index >= 0)
        return (arrived, jnp.where(storing, placed, finished))

    start_state = (
        jnp.zeros((row_count, width), jnp.bfloat16),
        jnp.zeros((batches, row_count, width), jnp.bfloat16),
    )
    last_arrival, finished = lax.fori_loop(0, batches + section_count - 1, relay_step, start_state)
    finished = spread_2(finished, "section", 0).reshape(batches * row_count, width)
    first_group = lax.axis_index("group") == 0
    outgoing = jnp.where(first_group, policy_hidden, finished)
    kept_rows = jnp.where(first_group, finished, policy_hidden)
    received = from_partner(outgoing, "group", 0)
    hidden_rows = jnp.where(
        first_group,
        jnp.concatenate([kept_rows, received], 0),
        jnp.concatenate([received, kept_rows], 0),
    )
    head_block = heads[0]
    logits = lax.psum_scatter(
        lax.dot_general(
            hidden_rows, head_block, (((1,), (1,)), ((), ())), preferred_element_type=jnp.float32
        ),
        "tensor",
        scatter_dimension=0,
        tiled=True,
    )
    paired = lax.all_to_all(logits[None], "group", split_axis=1, concat_axis=0, tiled=True)
    reference_logits = paired[0]
    policy_logits = paired[1]
    local_rows = policy_logits.shape[0]
    vocab_block = policy_logits.shape[1]
    row_start = (
        lax.axis_index("tensor") * lax.axis_size("group") + lax.axis_index("group")
    ) * local_rows
    vocab_ids = section_here * vocab_block + lax.iota(jnp.int32, vocab_block)
    wanted = lax.dynamic_slice_in_dim(sampled, row_start, local_rows, 0)
    hits = vocab_ids[None, :] == wanted[:, None]
    picked = jnp.sum(jnp.where(hits, policy_logits, 0.0), axis=1)
    peak_pol, peak_ref = lax.pmax(
        (jnp.max(policy_logits, axis=1), jnp.max(reference_logits, axis=1)), "section"
    )
    weights_pol = jnp.exp(policy_logits - peak_pol[:, None])
    weights_ref = jnp.exp(reference_logits - peak_ref[:, None])
    local_cross = jnp.sum(weights_pol * (policy_logits - reference_logits), axis=1)
    total_pol, total_ref, cross, chosen = lax.psum(
        (jnp.sum(weights_pol, axis=1), jnp.sum(weights_ref, axis=1), local_cross, picked), "section"
    )
    lse_pol = peak_pol + jnp.log(total_pol)
    lse_ref = peak_ref + jnp.log(total_ref)
    token_kl = cross / total_pol - lse_pol + lse_ref
    log_prob = chosen - lse_pol
    token_adv = lax.dynamic_slice_in_dim(
        jnp.repeat(advantages(rewards, prompt_ids), RLEN), row_start, local_rows, 0
    )
    live = lax.dynamic_slice_in_dim(live_mask, row_start, local_rows, 0).astype(jnp.float32)
    token_loss = live * (penalty * token_kl - token_adv * log_prob) / RLEN
    return (token_kl, token_loss)


def solution(mesh):
    in_specs = (
        P("group", None, None, "tensor"),
        P("section", "tensor"),
        P("section", "tensor", None),
        P("section", None, "tensor"),
        P("group", "tensor"),
        P("group", "section", "tensor"),
        P(),
        P(),
        P(),
        P(),
    )
    out_specs = (P(("tensor", "group")), P(("tensor", "group")))
    return jax.shard_map(shards, mesh=mesh, in_specs=in_specs, out_specs=out_specs, check_vma=False)
```

profile of v0, /device:TPU:1, one launch (start us, length us, event | category | flops | bytes accessed | tf_op | source)
XLA Modules:
  0.0 2076.6 jit_solution(47395482783940447)
XLA Ops:
  8.2 1720.4 %while.17 = (s32[]{:T(128)}, bf16[128,2048]{1,0:T(8,128)(2,1)S(1)}, bf16[2,128,2048]{2,1,0:T(8,128)(2,1)S(1)}, pred[]{:T(512)}, bf16[2,128,2048]{2,1,0:T(8,128)(...) while((s32[]{:T(128)}, bf16[128,2048]{1,0:T(8,128)(2,1)S(1)}, ...), condition=%wide.region_4.5_spmd, body=%wide.region_0.4_spmd.sunk | while | flops 607518976 | bytes 14691641 | solution.py:90
  27.9 64.5 %all-reduce.7.cloned.1.call-done = f32[128,768]{1,0:T(8,128)} async-done(((f32[128,768]{1,0:T(8,128)}), f32[128,768]{1,0:T(8,128)}) %all-reduce.7.cloned.1.call-update) | async-done | bytes 393232 | tf_op jit(solution)/shard_map/while/body/eval_jaxpr/psum | solution.py:66
  110.9 16.0 psum.70
  130.2 63.4 %all-reduce.7.cloned.1.call-done = f32[128,768]{1,0:T(8,128)} async-done(((f32[128,768]{1,0:T(8,128)}), f32[128,768]{1,0:T(8,128)}) %all-reduce.7.cloned.1.call-update) | async-done | bytes 393232 | tf_op jit(solution)/shard_map/while/body/eval_jaxpr/psum | solution.py:66
  231.4 63.4 %all-reduce.7.cloned.1.call-done = f32[128,768]{1,0:T(8,128)} async-done(((f32[128,768]{1,0:T(8,128)}), f32[128,768]{1,0:T(8,128)}) %all-reduce.7.cloned.1.call-update) | async-done | bytes 393232 | tf_op jit(solution)/shard_map/while/body/eval_jaxpr/psum | solution.py:66
  332.6 63.4 %all-reduce.7.cloned.1.call-done = f32[128,768]{1,0:T(8,128)} async-done(((f32[128,768]{1,0:T(8,128)}), f32[128,768]{1,0:T(8,128)}) %all-reduce.7.cloned.1.call-update) | async-done | bytes 393232 | tf_op jit(solution)/shard_map/while/body/eval_jaxpr/psum | solution.py:66
  433.8 63.4 %all-reduce.7.cloned.1.call-done = f32[128,768]{1,0:T(8,128)} async-done(((f32[128,768]{1,0:T(8,128)}), f32[128,768]{1,0:T(8,128)}) %all-reduce.7.cloned.1.call-update) | async-done | bytes 393232 | tf_op jit(solution)/shard_map/while/body/eval_jaxpr/psum | solution.py:66
  535.0 63.4 %all-reduce.7.cloned.1.call-done = f32[128,768]{1,0:T(8,128)} async-done(((f32[128,768]{1,0:T(8,128)}), f32[128,768]{1,0:T(8,128)}) %all-reduce.7.cloned.1.call-update) | async-done | bytes 393232 | tf_op jit(solution)/shard_map/while/body/eval_jaxpr/psum | solution.py:66
  636.2 63.4 %all-reduce.7.cloned.1.call-done = f32[128,768]{1,0:T(8,128)} async-done(((f32[128,768]{1,0:T(8,128)}), f32[128,768]{1,0:T(8,128)}) %all-reduce.7.cloned.1.call-update) | async-done | bytes 393232 | tf_op jit(solution)/shard_map/while/body/eval_jaxpr/psum | solution.py:66
  737.4 63.4 %all-reduce.7.cloned.1.call-done = f32[128,768]{1,0:T(8,128)} async-done(((f32[128,768]{1,0:T(8,128)}), f32[128,768]{1,0:T(8,128)}) %all-reduce.7.cloned.1.call-update) | async-done | bytes 393232 | tf_op jit(solution)/shard_map/while/body/eval_jaxpr/psum | solution.py:66
  838.6 63.4 %all-reduce.7.cloned.1.call-done = f32[128,768]{1,0:T(8,128)} async-done(((f32[128,768]{1,0:T(8,128)}), f32[128,768]{1,0:T(8,128)}) %all-reduce.7.cloned.1.call-update) | async-done | bytes 393232 | tf_op jit(solution)/shard_map/while/body/eval_jaxpr/psum | solution.py:66
  939.8 63.4 %all-reduce.7.cloned.1.call-done = f32[128,768]{1,0:T(8,128)} async-done(((f32[128,768]{1,0:T(8,128)}), f32[128,768]{1,0:T(8,128)}) %all-reduce.7.cloned.1.call-update) | async-done | bytes 393232 | tf_op jit(solution)/shard_map/while/body/eval_jaxpr/psum | solution.py:66
  1040.9 63.4 %all-reduce.7.cloned.1.call-done = f32[128,768]{1,0:T(8,128)} async-done(((f32[128,768]{1,0:T(8,128)}), f32[128,768]{1,0:T(8,128)}) %all-reduce.7.cloned.1.call-update) | async-done | bytes 393232 | tf_op jit(solution)/shard_map/while/body/eval_jaxpr/psum | solution.py:66
  1142.1 63.4 %all-reduce.7.cloned.1.call-done = f32[128,768]{1,0:T(8,128)} async-done(((f32[128,768]{1,0:T(8,128)}), f32[128,768]{1,0:T(8,128)}) %all-reduce.7.cloned.1.call-update) | async-done | bytes 393232 | tf_op jit(solution)/shard_map/while/body/eval_jaxpr/psum | solution.py:66
  1243.3 63.4 %all-reduce.7.cloned.1.call-done = f32[128,768]{1,0:T(8,128)} async-done(((f32[128,768]{1,0:T(8,128)}), f32[128,768]{1,0:T(8,128)}) %all-reduce.7.cloned.1.call-update) | async-done | bytes 393232 | tf_op jit(solution)/shard_map/while/body/eval_jaxpr/psum | solution.py:66
  1344.5 63.4 %all-reduce.7.cloned.1.call-done = f32[128,768]{1,0:T(8,128)} async-done(((f32[128,768]{1,0:T(8,128)}), f32[128,768]{1,0:T(8,128)}) %all-reduce.7.cloned.1.call-update) | async-done | bytes 393232 | tf_op jit(solution)/shard_map/while/body/eval_jaxpr/psum | solution.py:66
  1445.7 63.4 %all-reduce.7.cloned.1.call-done = f32[128,768]{1,0:T(8,128)} async-done(((f32[128,768]{1,0:T(8,128)}), f32[128,768]{1,0:T(8,128)}) %all-reduce.7.cloned.1.call-update) | async-done | bytes 393232 | tf_op jit(solution)/shard_map/while/body/eval_jaxpr/psum | solution.py:66
  1546.9 63.4 %all-reduce.7.cloned.1.call-done = f32[128,768]{1,0:T(8,128)} async-done(((f32[128,768]{1,0:T(8,128)}), f32[128,768]{1,0:T(8,128)}) %all-reduce.7.cloned.1.call-update) | async-done | bytes 393232 | tf_op jit(solution)/shard_map/while/body/eval_jaxpr/psum | solution.py:66
  1648.1 63.4 %all-reduce.7.cloned.1.call-done = f32[128,768]{1,0:T(8,128)} async-done(((f32[128,768]{1,0:T(8,128)}), f32[128,768]{1,0:T(8,128)}) %all-reduce.7.cloned.1.call-update) | async-done | bytes 393232 | tf_op jit(solution)/shard_map/while/body/eval_jaxpr/psum | solution.py:66
  1729.9 161.5 %all-reduce.5.cloned.1.call-done = bf16[256,2048]{1,0:T(8,128)(2,1)} async-done(((bf16[256,2048]{1,0:T(8,128)(2,1)}), bf16[256,2048]{1,0:T(8,128)(2,1)}) %all-reduce.5.cloned.1.call-update) | async-done | bytes 1048592 | tf_op jit(solution)/shard_map/psum | solution.py:21
  1896.1 44.9 %collective-permute-done.1 = bf16[256,2048]{1,0:T(8,128)(2,1)S(1)} collective-permute-done((bf16[256,2048]{1,0:T(8,128)(2,1)S(1)}, bf16[256,2048]{1,0:T(8,128)(2,1)S(1)}, u32[]{:S(2)}, u32[]{:S(2)}) %collective-permute-start.1) | collective-permute-done | bytes 1048608 | tf_op jit(solution)/shard_map/ppermute | solution.py:31
  1945.3 39.6 %reduce-scatter.2.cloned.1.call-done = f32[64,1024]{1,0:T(8,128)} async-done(((f32[512,1024]{1,0:T(8,128)}), f32[64,1024]{1,0:T(8,128)}) %reduce-scatter.2.cloned.1.call-update) | async-done | bytes 262160 | tf_op jit(solution)/shard_map/reduce_scatter | solution.py:102
  2001.7 35.0 %all-reduce.1 = (f32[32]{0:T(128)S(1)}, f32[32]{0:T(128)S(1)}) all-reduce(f32[32]{0:T(128)S(1)} %get-tuple-element.238, f32[32]{0:T(128)S(1)} %slice_reduce_fusion), channel_id=1, replica_groups=mesh['section'=16,'tensor'=8,'group'=2] {'section'}, use_global_device_ids=true, to_apply=%region_14.15 | all-reduce | flops 64 | bytes 512 | tf_op jit(solution)/shard_map/pmax | solution.py:122
  2036.9 31.3 %all-reduce = (f32[32]{0:T(128)S(1)}, f32[32]{0:T(128)S(1)}, f32[32]{0:T(128)S(1)}, f32[32]{0:T(128)S(1)}) all-reduce(f32[32]{0:T(128)S(1)} %get-tuple-element.206, f32[32]{0:T(128)S(1)} %get-tuple-element.204, f32[32]{0:T(128)S(1)} %get-tuple-element.203, ...), channel_id=1, replica_groups=mesh['section'=16,'tensor'=8,'group'=2] {'section'}, use_global_device_ids=true, to_apply=%region_16.17 | all-reduce | flops 128 | bytes 1024 | tf_op jit(solution)/shard_map/psum | solution.py:128
  (203 shorter events, 652.6 us)
Async XLA Ops:
  8.2 84.2 %all-reduce.7.cloned.1.call-start = ((), (), s32[]{:S(2)}) async-start(), calls=%async_computation.4 | async-start | bytes 786432 | tf_op jit(solution)/shard_map/while/body/eval_jaxpr/psum | solution.py:66
  109.5 84.1 %all-reduce.7.cloned.1.call-start = ((), (), s32[]{:S(2)}) async-start(), calls=%async_computation.4 | async-start | bytes 786432 | tf_op jit(solution)/shard_map/while/body/eval_jaxpr/psum | solution.py:66
  210.7 84.1 %all-reduce.7.cloned.1.call-start = ((), (), s32[]{:S(2)}) async-start(), calls=%async_computation.4 | async-start | bytes 786432 | tf_op jit(solution)/shard_map/while/body/eval_jaxpr/psum | solution.py:66
  296.9 14.8 collective-permute-start
  311.9 84.1 %all-reduce.7.cloned.1.call-start = ((), (), s32[]{:S(2)}) async-start(), calls=%async_computation.4 | async-start | bytes 786432 | tf_op jit(solution)/shard_map/while/body/eval_jaxpr/psum | solution.py:66
  413.1 84.1 %all-reduce.7.cloned.1.call-start = ((), (), s32[]{:S(2)}) async-start(), calls=%async_computation.4 | async-start | bytes 786432 | tf_op jit(solution)/shard_map/while/body/eval_jaxpr/psum | solution.py:66
  499.3 14.8 collective-permute-start
  514.3 84.1 %all-reduce.7.cloned.1.call-start = ((), (), s32[]{:S(2)}) async-start(), calls=%async_computation.4 | async-start | bytes 786432 | tf_op jit(solution)/shard_map/while/body/eval_jaxpr/psum | solution.py:66
  615.5 84.1 %all-reduce.7.cloned.1.call-start = ((), (), s32[]{:S(2)}) async-start(), calls=%async_computation.4 | async-start | bytes 786432 | tf_op jit(solution)/shard_map/while/body/eval_jaxpr/psum | solution.py:66
  701.7 14.8 collective-permute-start
  716.7 84.1 %all-reduce.7.cloned.1.call-start = ((), (), s32[]{:S(2)}) async-start(), calls=%async_computation.4 | async-start | bytes 786432 | tf_op jit(solution)/shard_map/while/body/eval_jaxpr/psum | solution.py:66
  817.9 84.1 %all-reduce.7.cloned.1.call-start = ((), (), s32[]{:S(2)}) async-start(), calls=%async_computation.4 | async-start | bytes 786432 | tf_op jit(solution)/shard_map/while/body/eval_jaxpr/psum | solution.py:66
  904.1 14.8 collective-permute-start
  919.1 84.1 %all-reduce.7.cloned.1.call-start = ((), (), s32[]{:S(2)}) async-start(), calls=%async_computation.4 | async-start | bytes 786432 | tf_op jit(solution)/shard_map/while/body/eval_jaxpr/psum | solution.py:66
  1020.3 84.1 %all-reduce.7.cloned.1.call-start = ((), (), s32[]{:S(2)}) async-start(), calls=%async_computation.4 | async-start | bytes 786432 | tf_op jit(solution)/shard_map/while/body/eval_jaxpr/psum | solution.py:66
  1121.5 84.1 %all-reduce.7.cloned.1.call-start = ((), (), s32[]{:S(2)}) async-start(), calls=%async_computation.4 | async-start | bytes 786432 | tf_op jit(solution)/shard_map/while/body/eval_jaxpr/psum | solution.py:66
  1222.7 84.1 %all-reduce.7.cloned.1.call-start = ((), (), s32[]{:S(2)}) async-start(), calls=%async_computation.4 | async-start | bytes 786432 | tf_op jit(solution)/shard_map/while/body/eval_jaxpr/psum | solution.py:66
  1323.9 84.1 %all-reduce.7.cloned.1.call-start = ((), (), s32[]{:S(2)}) async-start(), calls=%async_computation.4 | async-start | bytes 786432 | tf_op jit(solution)/shard_map/while/body/eval_jaxpr/psum | solution.py:66
  1425.1 84.1 %all-reduce.7.cloned.1.call-start = ((), (), s32[]{:S(2)}) async-start(), calls=%async_computation.4 | async-start | bytes 786432 | tf_op jit(solution)/shard_map/while/body/eval_jaxpr/psum | solution.py:66
  1526.2 84.1 %all-reduce.7.cloned.1.call-start = ((), (), s32[]{:S(2)}) async-start(), calls=%async_computation.4 | async-start | bytes 786432 | tf_op jit(solution)/shard_map/while/body/eval_jaxpr/psum | solution.py:66
  1627.4 84.1 %all-reduce.7.cloned.1.call-start = ((), (), s32[]{:S(2)}) async-start(), calls=%async_computation.4 | async-start | bytes 786432 | tf_op jit(solution)/shard_map/while/body/eval_jaxpr/psum | solution.py:66
  1728.6 162.7 %all-reduce.5.cloned.1.call-start = ((), (), s32[]{:S(2)}) async-start(), calls=%async_computation.2 | async-start | bytes 2097152 | tf_op jit(solution)/shard_map/psum | solution.py:21
  1729.8 255.0 %reduce-scatter.2.cloned.1.call-start = ((), (), s32[]{:S(2)}) async-start(), calls=%async_computation.3 | async-start | bytes 2359296 | tf_op jit(solution)/shard_map/reduce_scatter | solution.py:102
  1892.9 48.2 %collective-permute-start.1 = (bf16[256,2048]{1,0:T(8,128)(2,1)S(1)}, bf16[256,2048]{1,0:T(8,128)(2,1)S(1)}, u32[]{:S(2)}, u32[]{:S(2)}) collective-permute-start(bf16[256,2048]{1,0:T(8,128)(2,1)S(1)} %get-tuple-element.236), channel_id=1, source_target_pairs={{0,1},{1,0},{2,3},{3,2},{4,5},{5,4},{6,7},{7,6},{8,9},{9,8},{10,11... | collective-permute-start | bytes 3145736 | tf_op jit(solution)/shard_map/ppermute | solution.py:31
  (18 other events, 427.0 us)
Sparse Core Ops, SparseCore 0:
  28.0 64.3 all-reduce.6
  130.3 63.2 all-reduce.6
  231.5 63.2 all-reduce.6
  332.7 63.2 all-reduce.6
  433.9 63.2 all-reduce.6
  535.1 63.2 all-reduce.6
  636.3 63.2 all-reduce.6
  737.5 63.2 all-reduce.6
  838.7 63.2 all-reduce.6
  939.9 63.2 all-reduce.6
  1041.1 63.2 all-reduce.6
  1142.3 63.2 all-reduce.6
  1243.5 63.2 all-reduce.6
  1344.7 63.2 all-reduce.6
  1445.9 63.2 all-reduce.6
  1547.0 63.2 all-reduce.6
  1648.2 63.2 all-reduce.6
Sparse Core Ops, SparseCore 1:
  1731.7 159.6 all-reduce.4
  1944.9 39.9 reduce-scatter.1
where the time goes:
time: 2100 us; the launch traced here: 2080 us
  waiting for transfers between devices  1560 us (74%)
  blocking collectives  337 us (16%)
  matrix products  94.8 us (5%)
  starting transfers between devices  33.6 us (2%)
  other arithmetic  30.3 us (1%)
    psum x17, waiting for transfers between devices, apply_layer(): summed = lax.psum(mixed, 'tensor')  1080 us
    psum x17, blocking collectives, apply_layer(): squares = lax.psum(jnp.sum(values * values, axis=1), 'tensor') / full_width  271 us
    ppermute x17, waiting for transfers between devices, from_behind(): return lax.ppermute(value, axis, pairs)  229 us
    psum x1, waiting for transfers between devices, spread_2(): return lax.psum(jnp.where(mine, x, jnp.zeros_like(x)), axis)  161 us
    dot_general x17, matrix products, apply_layer(): mixed = jnp.dot(normed, weight_in, preferred_element_type=jnp.float32)  55.9 us
    ppermute x1, waiting for transfers between devices, from_partner(): return lax.ppermute(block, axis, route)  44.9 us
  transfers between devices with their start and end apart: 38, of which 38 were waited for; matrix products, arithmetic and copies ran while one was open for 0% of the time, Pallas kernels for 0%

commit v1 on v0

v1 whole, which is shorter than its diff:
```python
import functools

import jax
import jax.numpy as jnp
from jax import lax
from jax.experimental import pallas as pl
from jax.experimental.pallas import tpu as pltpu
from jax.sharding import PartitionSpec as P

RLEN = 64
ROWS = 16
HALF = 8
SIDE = 4

epsilon = 1e-05
penalty = 0.04
MESH = pl.DeviceIdType.MESH


def as_count(flag):
    return jnp.where(flag, 1, 0).astype(jnp.int32)


def tree_edges(section, group):
    last = SIDE - 1
    row, column = section // SIDE, section % SIDE

    def at(r, c):
        return jnp.logical_and(row == r, column == c)

    def tree(mirror):
        place = (lambda c: last - c) if mirror else (lambda c: c)
        step = 1 if mirror else -1

        def here(r, c):
            return at(r, place(c))

        def any_of(spots):
            flag = here(*spots[0])
            for spot in spots[1:]:
                flag = jnp.logical_or(flag, here(*spot))
            return flag

        low_rows = row < last
        along = (
            jnp.logical_or(
                jnp.logical_and(low_rows, column != place(0)),
                here(last, last),
            ),
            section + step,
            jnp.logical_or(
                jnp.logical_and(low_rows, column != place(last)),
                here(last, last - 1),
            ),
            section - step,
        )
        up = (
            any_of([(3, 3), (0, 3), (2, 1), (2, 0)]),
            ((row + 1) % SIDE) * SIDE + column,
            any_of([(0, 3), (1, 3), (3, 1), (3, 0)]),
            ((row + SIDE - 1) % SIDE) * SIDE + column,
        )
        down = (
            here(3, 3),
            ((row + SIDE - 1) % SIDE) * SIDE + column,
            here(2, 3),
            ((row + 1) % SIDE) * SIDE + column,
        )
        return [along, up, down]

    return tree(False), tree(True)


def relay_kernel(
    x_ref, gain_ref, win_ref, wout_ref, out_ref,
    stream, partial, pieces, mine, twin_rows, leaving,
    piece_send, piece_recv, twin_send, twin_recv, stream_send, stream_recv, final_send, final_recv,
):
    batches = x_ref.shape[0]
    width = x_ref.shape[2]
    units = wout_ref.shape[0]
    tensor_count = lax.axis_size("tensor")
    section_count = lax.axis_size("section")
    section = lax.axis_index("section")
    tensor = lax.axis_index("tensor")
    group = lax.axis_index("group")
    core = tensor % 2
    twin = tensor + 1 - 2 * core
    first_section = section == 0
    last_section = section == section_count - 1
    in_first = group == 0
    tree_a, tree_b = tree_edges(section, group)
    entry = SIDE * (SIDE - 1)
    crossing_out = jnp.logical_and(last_section, group == 1)
    crossing_in = jnp.logical_and(section == entry, in_first)

    barrier = pltpu.get_barrier_semaphore()
    expected = jnp.int32(tensor_count - 1)
    for offset in range(1, tensor_count):
        pl.semaphore_signal(
            barrier, 1, device_id={"tensor": (tensor + offset) % tensor_count}, device_id_type=MESH
        )

    def greet(flag, where):
        @pl.when(flag)
        def _():
            pl.semaphore_signal(barrier, 1, device_id=where, device_id_type=MESH)

        return as_count(flag)

    expected += greet(jnp.logical_not(last_section), {"section": section + 1})
    expected += greet(jnp.logical_not(first_section), {"section": section - 1})
    for sends, target, receives, source in tree_a + tree_b:
        expected += greet(jnp.logical_and(in_first, sends), {"section": target})
        expected += greet(jnp.logical_and(in_first, receives), {"section": source})
    expected += greet(crossing_out, {"section": entry, "group": 0})
    expected += greet(crossing_in, {"section": section_count - 1, "group": 1})
    pl.semaphore_wait(barrier, expected)

    def piece_copy(batch, offset):
        target = (tensor + offset) % tensor_count
        return pltpu.make_async_remote_copy(
            src_ref=partial.at[batch, target % 2],
            dst_ref=pieces.at[batch, offset - 1],
            send_sem=piece_send.at[batch],
            recv_sem=piece_recv.at[batch],
            device_id={"tensor": target},
            device_id_type=MESH,
        )

    def twin_copy(batch):
        return pltpu.make_async_remote_copy(
            src_ref=mine.at[batch],
            dst_ref=twin_rows.at[batch],
            send_sem=twin_send.at[batch],
            recv_sem=twin_recv.at[batch],
            device_id={"tensor": twin},
            device_id_type=MESH,
        )

    def stream_copy(batch):
        return pltpu.make_async_remote_copy(
            src_ref=leaving.at[batch],
            dst_ref=stream.at[batch],
            send_sem=stream_send.at[batch],
            recv_sem=stream_recv.at[batch],
            device_id={"section": section + 1},
            device_id_type=MESH,
        )

    def final_copy(source, slot, edge, where):
        return pltpu.make_async_remote_copy(
            src_ref=source,
            dst_ref=out_ref.at[slot],
            send_sem=final_send.at[slot, edge],
            recv_sem=final_recv.at[slot],
            device_id=where,
            device_id_type=MESH,
        )

    def stage_a(batch):
        @pl.when(first_section)
        def _():
            stream[batch] = x_ref[batch]

        @pl.when(jnp.logical_not(first_section))
        def _():
            stream_copy(batch).wait_recv()

        values = stream[batch].astype(jnp.float32)
        squares = jnp.sum(values * values, axis=1, keepdims=True)
        scaled = (values * gain_ref[...]).astype(jnp.bfloat16)
        mixed = jnp.dot(scaled, win_ref[...], preferred_element_type=jnp.float32)
        squares = jnp.broadcast_to(squares, (ROWS, 128))
        coarse = squares.astype(jnp.bfloat16).astype(jnp.float32)
        fine = squares - coarse
        for half in range(2):
            rows = slice(half * HALF, (half + 1) * HALF)
            partial[batch, half, :, :units] = jnp.concatenate(
                [mixed[rows, :units], mixed[rows, units:]], 0
            ).astype(jnp.bfloat16)
            partial[batch, half, :, units:] = jnp.concatenate(
                [coarse[rows], fine[rows]], 0
            ).astype(jnp.bfloat16)
        for offset in range(1, tensor_count):
            piece_copy(batch, offset).start()

    def stage_b(batch):
        pltpu.make_async_copy(pieces.at[batch], pieces.at[batch], piece_recv.at[batch]).wait()
        total = partial[batch, core].astype(jnp.float32)
        for offset in range(1, tensor_count):
            total += pieces[batch, offset - 1].astype(jnp.float32)
        squares = total[:HALF, units:units + 1] + total[HALF:, units:units + 1]
        scale = lax.rsqrt(squares / (width * tensor_count) + epsilon)
        gate = total[:HALF, :units] * scale
        up = total[HALF:, :units] * scale
        mine[batch] = gate / (1.0 + jnp.exp(-gate)) * up
        twin_copy(batch).start()

    def stage_c(batch):
        twin_copy(batch).wait_recv()
        here, there = mine[batch], twin_rows[batch]
        hidden = jnp.concatenate(
            [jnp.where(core == 0, here, there), jnp.where(core == 0, there, here)], 0
        ).astype(jnp.bfloat16)
        update = jnp.dot(hidden, wout_ref[...], preferred_element_type=jnp.float32)
        leaving[batch] = (stream[batch].astype(jnp.float32) + update).astype(jnp.bfloat16)

        @pl.when(jnp.logical_not(last_section))
        def _():
            stream_copy(batch).start()

        @pl.when(jnp.logical_and(last_section, in_first))
        def _():
            out_ref[batch] = leaving[batch]
            for edge, (_, target, _, _) in enumerate(tree_a):
                final_copy(leaving.at[batch], batch, edge, {"section": target}).start()

        @pl.when(crossing_out)
        def _():
            final_copy(
                leaving.at[batch], batches + batch, 0, {"section": entry, "group": 0}
            ).start()

    def step(index, carry):
        @pl.when(index < batches)
        def _():
            stage_a(index)

        @pl.when(index >= 2)
        def _():
            stage_c(index - 2)

        @pl.when(jnp.logical_and(index >= 1, index <= batches))
        def _():
            stage_b(index - 1)

        return carry

    lax.fori_loop(0, batches + 2, step, 0)

    def forward(batch, carry):
        for first, edges in ((0, tree_a), (batches, tree_b)):
            slot = first + batch
            root = jnp.logical_and(last_section, first == 0)

            @pl.when(jnp.logical_and(in_first, jnp.logical_not(root)))
            def _(slot=slot, edges=edges):
                pltpu.make_async_copy(
                    out_ref.at[slot], out_ref.at[slot], final_recv.at[slot]
                ).wait()
                for edge, (sends, target, _, _) in enumerate(edges):
                    @pl.when(sends)
                    def _(edge=edge, target=target):
                        final_copy(out_ref.at[slot], slot, edge, {"section": target}).start()

        return carry

    lax.fori_loop(0, batches, forward, 0)

    def drain(batch, carry):
        pltpu.make_async_copy(pieces.at[batch], pieces.at[batch], piece_send.at[batch]).wait()
        twin_copy(batch).wait_send()

        @pl.when(jnp.logical_not(last_section))
        def _():
            stream_copy(batch).wait_send()

        for first, edges in ((0, tree_a), (batches, tree_b)):
            slot = first + batch
            for edge, (sends, target, _, _) in enumerate(edges):
                @pl.when(jnp.logical_and(in_first, sends))
                def _(edge=edge, target=target, slot=slot):
                    final_copy(out_ref.at[slot], slot, edge, {"section": target}).wait_send()

        @pl.when(crossing_out)
        def _():
            final_copy(
                leaving.at[batch], batches + batch, 0, {"section": entry, "group": 0}
            ).wait_send()

        return carry

    lax.fori_loop(0, batches, drain, 0)


def relay(rows, gain, weight_in, weight_out):
    tensor_count = lax.axis_size("tensor")
    batches, _, width = rows.shape
    units = weight_out.shape[0]
    piece = (ROWS, units + 128)
    dma = pltpu.SemaphoreType.DMA
    vmem = pl.BlockSpec(memory_space=pltpu.VMEM)
    return pl.pallas_call(
        relay_kernel,
        out_shape=jax.ShapeDtypeStruct((2 * batches, ROWS, width), jnp.bfloat16),
        in_specs=[vmem] * 4,
        out_specs=vmem,
        scratch_shapes=[
            pltpu.VMEM((batches, ROWS, width), jnp.bfloat16),
            pltpu.VMEM((batches, 2) + piece, jnp.bfloat16),
            pltpu.VMEM((batches, tensor_count - 1) + piece, jnp.bfloat16),
            pltpu.VMEM((batches, HALF, units), jnp.float32),
            pltpu.VMEM((batches, HALF, units), jnp.float32),
            pltpu.VMEM((batches, ROWS, width), jnp.bfloat16),
            dma((batches,)),
            dma((batches,)),
            dma((batches,)),
            dma((batches,)),
            dma((batches,)),
            dma((batches,)),
            dma((2 * batches, 3)),
            dma((2 * batches,)),
        ],
        compiler_params=pltpu.CompilerParams(
            collective_id=0, has_side_effects=True, vmem_limit_bytes=40 * 1024 * 1024
        ),
        name="relay",
    )(rows, gain, weight_in, weight_out)


def from_partner(block, axis):
    return lax.ppermute(block, axis, [(0, 1), (1, 0)])


def advantages(rewards, prompt_ids):
    same = (prompt_ids[:, None] == prompt_ids[None, :]).astype(jnp.float32)
    counts = jnp.sum(same, axis=1)
    means = jnp.sum(same * rewards[None, :], axis=1) / counts
    spread = rewards[None, :] - means[:, None]
    variance = jnp.sum(same * spread * spread, axis=1) / counts
    return (rewards - means) / jnp.maximum(jnp.sqrt(variance), 1.0)


def shards(
    ref_input, norm_gain, w_in, w_out, policy_hidden, heads, sampled, live_mask, rewards, prompt_ids
):
    section_here = lax.axis_index("section")
    group_here = lax.axis_index("group")
    first_group = group_here == 0
    width = ref_input.shape[3]
    rows = ref_input.reshape(-1, ROWS, width)
    policy_other = lax.ppermute(policy_hidden, "group", [(0, 1)])
    policy_rows = jnp.concatenate([policy_other, policy_hidden], 0)
    final = relay(rows, norm_gain, w_in[0], w_out[0]).reshape(-1, width)
    hidden_rows = jnp.where(first_group, final, policy_rows)
    logits = lax.psum_scatter(
        lax.dot_general(
            hidden_rows, heads[0], (((1,), (1,)), ((), ())), preferred_element_type=jnp.float32
        ),
        "tensor",
        scatter_dimension=0,
        tiled=True,
    )
    paired = lax.all_to_all(logits[None], "group", split_axis=1, concat_axis=0, tiled=True)
    reference_logits = paired[0]
    policy_logits = paired[1]
    local_rows = policy_logits.shape[0]
    vocab_block = policy_logits.shape[1]
    row_start = (lax.axis_index("tensor") * lax.axis_size("group") + group_here) * local_rows
    vocab_ids = section_here * vocab_block + lax.iota(jnp.int32, vocab_block)
    wanted = lax.dynamic_slice_in_dim(sampled, row_start, local_rows, 0)
    hits = vocab_ids[None, :] == wanted[:, None]
    picked = jnp.sum(jnp.where(hits, policy_logits, 0.0), axis=1)
    near_pol = jnp.max(policy_logits, axis=1)
    near_ref = jnp.max(reference_logits, axis=1)
    weights_pol = jnp.exp(policy_logits - near_pol[:, None])
    weights_ref = jnp.exp(reference_logits - near_ref[:, None])
    local_cross = jnp.sum(weights_pol * (policy_logits - reference_logits), axis=1)
    stats = jnp.stack(
        [near_pol, near_ref, jnp.sum(weights_pol, axis=1), jnp.sum(weights_ref, axis=1), local_cross, picked]
    )
    stats = lax.all_gather(stats, "section")
    peak_pol = jnp.max(stats[:, 0], axis=0)
    peak_ref = jnp.max(stats[:, 1], axis=0)
    shift_pol = jnp.exp(stats[:, 0] - peak_pol)
    shift_ref = jnp.exp(stats[:, 1] - peak_ref)
    total_pol = jnp.sum(shift_pol * stats[:, 2], axis=0)
    total_ref = jnp.sum(shift_ref * stats[:, 3], axis=0)
    cross = jnp.sum(shift_pol * stats[:, 4], axis=0)
    chosen = jnp.sum(stats[:, 5], axis=0)
    lse_pol = peak_pol + jnp.log(total_pol)
    lse_ref = peak_ref + jnp.log(total_ref)
    token_kl = cross / total_pol - lse_pol + lse_ref
    log_prob = chosen - lse_pol
    token_adv = lax.dynamic_slice_in_dim(
        jnp.repeat(advantages(rewards, prompt_ids), RLEN), row_start, local_rows, 0
    )
    live = lax.dynamic_slice_in_dim(live_mask, row_start, local_rows, 0).astype(jnp.float32)
    token_loss = live * (penalty * token_kl - token_adv * log_prob) / RLEN
    return (token_kl, token_loss)


def solution(mesh):
    in_specs = (
        P("group", None, None, "tensor"),
        P("section", "tensor"),
        P("section", "tensor", None),
        P("section", None, "tensor"),
        P("group", "tensor"),
        P("group", "section", "tensor"),
        P(),
        P(),
        P(),
        P(),
    )
    out_specs = (P(("tensor", "group")), P(("tensor", "group")))
    return jax.shard_map(shards, mesh=mesh, in_specs=in_specs, out_specs=out_specs, check_vma=False)
```

time: 2100 us -> 723 us (0.34)
  waiting for transfers between devices: 1560 us -> 152 us
  Pallas kernels: 0 us -> 478 us
  blocking collectives: 337 us -> 34.3 us
  matrix products: 94.8 us -> 3.71 us
  other arithmetic: 30.3 us -> 2.95 us
    psum x18 -> x0, waiting for transfers between devices: 1240 us -> none  [the longest x17 1080 us: apply_layer(): summed = lax.psum(mixed, 'tensor')]
    pallas_call x0 -> x1, Pallas kernels: none -> 478 us  [relay(): pl.pallas_call(relay_kernel, out_shape=jax.ShapeDtypeStruct((2 * batches,...]
    psum x18 -> x0, blocking collectives: 302 us -> none  [the longest x17 271 us: apply_layer(): squares = lax.psum(jnp.sum(values * values, axis=1), 'tensor') / full_width]
    ppermute x18 -> x1, waiting for transfers between devices: 274 us -> 0.01 us  [shards(): policy_other = lax.ppermute(policy_hidden, 'group', [(0, 1)])]
    reduce_scatter x1, waiting for transfers between devices: 39.6 us -> 145 us  [shards(): lax.psum_scatter(lax.dot_general(hidden_rows, heads[0], (((1,), (1,)), ((...]
    dot_general x35 -> x1, matrix products: 94.8 us -> 3.71 us  [shards(): lax.dot_general(hidden_rows, heads[0], (((1,), (1,)), ((), ())), preferre...]
    pmax x1 -> x0, blocking collectives: 35 us -> none  [shards(): lax.pmax((jnp.max(policy_logits, axis=1), jnp.max(reference_logits, axis=...]
    all_gather x0 -> x1, blocking collectives: none -> 34.3 us  [shards(): stats = lax.all_gather(stats, 'section')]
  transfers between devices with their start and end apart: 38 -> 3, of which waited for: 38 -> 2; matrix products, arithmetic and copies ran while one was open for 0% -> 0% of each run, Pallas kernels for 0% -> 67%
where the time goes in v1:
time: 723 us; the launch traced here: 712 us
  Pallas kernels  478 us (66%)
  waiting for transfers between devices  152 us (21%)
  blocking collectives  34.3 us (5%)
  starting transfers between devices  16.1 us (2%)
  between operations  14.1 us (2%)
  local copies, waits for them, and re-layouts  10.7 us (1%)
    pallas_call x1, Pallas kernels, relay(): pl.pallas_call(relay_kernel, out_shape=jax.ShapeDtypeStruct((2 * batches,...  478 us
    reduce_scatter x1, waiting for transfers between devices, shards(): lax.psum_scatter(lax.dot_general(hidden_rows, heads[0], (((1,), (1,)), ((...  145 us
    all_gather x1, blocking collectives, shards(): stats = lax.all_gather(stats, 'section')  34.3 us
  transfers between devices with their start and end apart: 3, of which 2 were waited for; matrix products, arithmetic and copies ran while one was open for 0% of the time, Pallas kernels for 67%

profile of v1, /device:TPU:1, one launch (start us, length us, event | category | flops | bytes accessed | tf_op | source)
XLA Modules:
  0.0 712.1 jit_solution(12681482435676792520)
XLA Ops:
  7.2 9.7 %collective-permute-start = (bf16[256,2048]{1,0:T(8,128)(2,1)}, bf16[256,2048]{1,0:T(8,128)(2,1)S(1)}, u32[]{:S(2)}, u32[]{:S(2)}) collective-permute-start(bf16[256,2048]{1,0:T(8,128)(2,1)} %param.14), channel_id=1, source_target_pairs={{0,1},{2,3},{4,5},{6,7},{8,9},{10,11},{12,13},{14,15},{16,17},{18,... | collective-permute-start | bytes 3145736 | tf_op jit(solution)/shard_map/ppermute | solution.py:343
  16.9 1.9 copy-done
  18.8 1.4 copy-done.1
  20.2 1.2 copy-done.2
  21.5 0.7 copy-done.3
  22.2 478.0 %relay.1 = bf16[32,16,2048]{2,1,0:T(8,128)(2,1)S(1)} custom-call(bf16[16,16,2048]{2,1,0:T(8,128)(2,1)S(1)} %bitcast.54, f32[1,2048]{1,0:T(1,128)S(1)} %copy-done.3, bf16[2048,768]{1,0:T(8,128)(2,1)S(1)} %bitcast.52, bf16[384,2048]{1,0:T(8,128)(2,1)S(1)} %bitcast.53), custom_call_target="tpu_custom_call" | custom-call | tf_op jit(solution)/shard_map/relay/pallas_call | solution.py:294
  500.1 0.2 pad_maximum_fusion
  500.3 0.3 broadcast_select_fusion
  500.6 1.9 copy-done.7
  502.5 3.7 fusion
  506.3 0.6 copy-done.5
  506.9 0.2 fusion.12
  507.1 0.2 fusion.10
  507.3 145.2 %reduce-scatter.2.cloned.1.call-done = f32[64,1024]{1,0:T(8,128)} async-done(((f32[512,1024]{1,0:T(8,128)}), f32[64,1024]{1,0:T(8,128)}) %reduce-scatter.2.cloned.1.call-update) | async-done | bytes 262160 | tf_op jit(solution)/shard_map/reduce_scatter | solution.py:347
  652.5 1.9 copy.19
  654.4 6.4 all-to-all-start
  660.9 0.1 reshape.38
  661.0 0.8 dynamic_slice.9
  661.7 7.0 all-to-all-done
  668.8 0.1 slice_reduce_fusion
  668.9 0.3 fusion.13
  669.3 0.3 fusion.5
  669.5 34.3 %all-gather.1 = f32[16,6,32]{2,1,0:T(8,128)S(1)} all-gather(f32[1,6,32]{2,1,0:T(8,128)S(1)} %bitcast.67), channel_id=2, replica_groups=mesh['section'=16,'tensor'=8,'group'=2] {'section'}, dimensions={0}, use_global_device_ids=true | all-gather | bytes 13056 | tf_op jit(solution)/shard_map/all_gather | solution.py:373
  704.0 1.3 multiply_multiply_fusion
  (23 shorter events, 0.4 us)
Async XLA Ops:
  7.2 645.3 %reduce-scatter.2.cloned.1.call-start = ((), (), s32[]{:S(2)}) async-start(), calls=%async_computation.2 | async-start | bytes 2359296 | tf_op jit(solution)/shard_map/reduce_scatter | solution.py:347
  7.2 492.9 %collective-permute-start = (bf16[256,2048]{1,0:T(8,128)(2,1)}, bf16[256,2048]{1,0:T(8,128)(2,1)S(1)}, u32[]{:S(2)}, u32[]{:S(2)}) collective-permute-start(bf16[256,2048]{1,0:T(8,128)(2,1)} %param.14), channel_id=1, source_target_pairs={{0,1},{2,3},{4,5},{6,7},{8,9},{10,11},{12,13},{14,15},{16,17},{18,... | collective-permute-start | bytes 3145736 | tf_op jit(solution)/shard_map/ppermute | solution.py:343
  16.9 1.9 copy-start
  18.8 1.4 copy-start.1
  20.2 1.2 copy-start.2
  21.5 0.7 copy-start.3
  22.2 478.0 %copy-start.4 = (bf16[256,2048]{1,0:T(8,128)(2,1)S(1)}, bf16[256,2048]{1,0:T(8,128)(2,1)}, u32[]{:S(2)}) copy-start(bf16[256,2048]{1,0:T(8,128)(2,1)} %param.14) | copy-start | bytes 3145732
  500.3 2.2 copy-start.7
  506.2 0.7 copy-start.5
  506.2 0.7 copy-start.6
  654.4 14.3 %all-to-all-start = ((f32[1,64,1024]{2,0,1:T(1,128)}), f32[1,64,1024]{2,0,1:T(1,128)S(1)}, u32[]{:S(2)}, u32[]{:S(2)}) async-start(f32[1,64,1024]{2,0,1:T(1,128)} %copy.19), calls=%async_computation.1 | async-start | bytes 524288 | tf_op jit(solution)/shard_map/all_to_all | solution.py:355
Sparse Core Ops, SparseCore 0:
  506.4 146.0 reduce-scatter.1

commit v2 on v1

v2 whole, which is shorter than its diff:
```python
import jax
import jax.numpy as jnp
from jax import lax
from jax.experimental import pallas as pl
from jax.experimental.pallas import tpu as pltpu
from jax.sharding import PartitionSpec as P

RLEN = 64
SIDE = 4
BLOCK = 16
ROWS = 32
HALF = ROWS // 2
PER = ROWS // BLOCK
CHUNK = 64
LANES = 128

epsilon = 1e-05
penalty = 0.04
MESH = pl.DeviceIdType.MESH


def as_count(flag):
    return jnp.where(flag, 1, 0).astype(jnp.int32)


def block_at(place):
    return (place % SIDE) * SIDE + place // SIDE


def tree_edges(section, mirror):
    last = SIDE - 1
    row, column = section // SIDE, section % SIDE
    far = column if mirror else last - column
    step = 1 if mirror else -1

    def any_of(spots):
        flag = jnp.bool_(False)
        for r, f in spots:
            flag = jnp.logical_or(flag, jnp.logical_and(row == r, far == f))
        return flag

    along = jnp.logical_or(jnp.logical_and(row < last, far < last), any_of([(3, 0)]))
    above = ((row + 1) % SIDE) * SIDE + column
    below = ((row + SIDE - 1) % SIDE) * SIDE + column
    edges = [
        (along, section + step),
        (any_of([(3, 0), (0, 0), (2, 2), (2, 3)]), above),
        (any_of([(3, 0)]), below),
    ]
    start = jnp.where(row == 1, 2, 1)
    depth = jnp.where(row == last, jnp.where(far < 2, far, far + 2), start + far)
    return edges, depth


def kernel(
    x_ref, gain_ref, win_hbm, wout_hbm, policy_ref, head_hbm, wanted_ref, out_ref,
    win_ref, wout_ref, head_ref,
    stream, partial, pieces, mine, twin_rows, leaving, final,
    logit_out, logit_in, pol_out, pol_in, stat_rows, stat_out, stat_in,
    load_sem, piece_send, piece_recv, twin_send, twin_recv, stream_send, stream_recv,
    final_send, final_recv, policy_send, logit_send, logit_recv, pol_send, pol_recv,
    stat_send, stat_recv,
):
    batches = stream.shape[0]
    width = stream.shape[2]
    units = wout_ref.shape[0]
    vocab_block = head_ref.shape[0]
    chunks = logit_out.shape[0]
    tensor_count = lax.axis_size("tensor")
    section_count = lax.axis_size("section")
    section = lax.axis_index("section")
    tensor = lax.axis_index("tensor")
    group = lax.axis_index("group")
    core = tensor % 2
    twin = tensor + 1 - 2 * core
    first_section = section == 0
    last_section = section == section_count - 1
    in_first = group == 0
    in_second = group == 1
    late_half = section >= section_count // 2
    entry = SIDE * (SIDE - 1)
    edges_a, depth_a = tree_edges(section, False)
    edges_b, depth_b = tree_edges(section, True)
    lag = depth_b + 1 - depth_a
    lag_a = jnp.where(in_first, jnp.maximum(-lag, 0), 0)
    lag_b = jnp.where(in_first, jnp.maximum(lag, 0), 0)
    lag_most = jnp.maximum(lag_a, lag_b)
    lag_limit = 6
    crossing_out = jnp.logical_and(last_section, in_second)

    loads = [
        pltpu.make_async_copy(win_hbm, win_ref, load_sem.at[0]),
        pltpu.make_async_copy(wout_hbm, wout_ref, load_sem.at[1]),
        pltpu.make_async_copy(head_hbm, head_ref, load_sem.at[2]),
    ]

    def own_block(source, target, place, sem):
        return pltpu.make_async_copy(
            source.at[block_at(place)],
            target.at[place // PER, pl.ds((place % PER) * BLOCK, BLOCK)],
            sem.at[place // PER],
        )

    places = batches * PER

    @pl.when(first_section)
    def _():
        def fetch(place, carry):
            own_block(x_ref, stream, place, stream_recv).start()
            return carry

        lax.fori_loop(0, places, fetch, 0)

    for load in loads:
        load.start()

    @pl.when(in_second)
    def _():
        def fetch(place, carry):
            pltpu.make_async_copy(
                policy_ref.at[block_at(place)],
                final.at[batches + place // PER, pl.ds((place % PER) * BLOCK, BLOCK)],
                final_recv.at[batches + place // PER],
            ).start()
            return carry

        lax.fori_loop(0, places, fetch, 0)

    stat_rows[...] = jnp.zeros_like(stat_rows)

    barrier = pltpu.get_barrier_semaphore()

    def greet(where):
        pl.semaphore_signal(barrier, 1, device_id=where, device_id_type=MESH)

    for offset in range(1, tensor_count):
        greet({"tensor": (tensor + offset) % tensor_count})
    for offset in range(section_count):
        greet({"section": (section + offset) % section_count, "group": 1 - group})

    @pl.when(in_first)
    def _():
        for offset in range(1, section_count):
            greet({"section": (section + offset) % section_count})

    @pl.when(jnp.logical_and(in_second, jnp.logical_not(first_section)))
    def _():
        greet({"section": section - 1})

    @pl.when(jnp.logical_and(in_second, jnp.logical_not(last_section)))
    def _():
        greet({"section": section + 1})

    neighbours = as_count(jnp.logical_not(first_section)) + as_count(jnp.logical_not(last_section))
    pl.semaphore_wait(
        barrier,
        tensor_count - 1 + section_count + jnp.where(in_first, section_count - 1, neighbours),
    )

    def policy_copy(place):
        return pltpu.make_async_remote_copy(
            src_ref=policy_ref.at[block_at(place)],
            dst_ref=final.at[place // PER, pl.ds((place % PER) * BLOCK, BLOCK)],
            send_sem=policy_send.at[place],
            recv_sem=final_recv.at[place // PER],
            device_id={"group": 1 - group},
            device_id_type=MESH,
        )

    def send_policy():
        def one(place, carry):
            policy_copy(place).start()
            return carry

        lax.fori_loop(0, places, one, 0)

    def piece_copy(batch, offset):
        target = (tensor + offset) % tensor_count
        return pltpu.make_async_remote_copy(
            src_ref=partial.at[batch, target % 2],
            dst_ref=pieces.at[batch, offset - 1],
            send_sem=piece_send.at[batch],
            recv_sem=piece_recv.at[batch],
            device_id={"tensor": target},
            device_id_type=MESH,
        )

    def twin_copy(batch):
        return pltpu.make_async_remote_copy(
            src_ref=mine.at[batch],
            dst_ref=twin_rows.at[batch],
            send_sem=twin_send.at[batch],
            recv_sem=twin_recv.at[batch],
            device_id={"tensor": twin},
            device_id_type=MESH,
        )

    def stream_copy(batch):
        return pltpu.make_async_remote_copy(
            src_ref=leaving.at[batch],
            dst_ref=stream.at[batch],
            send_sem=stream_send.at[batch],
            recv_sem=stream_recv.at[batch],
            device_id={"section": section + 1},
            device_id_type=MESH,
        )

    def final_copy(source, slot, edge, where):
        return pltpu.make_async_remote_copy(
            src_ref=source,
            dst_ref=final.at[slot],
            send_sem=final_send.at[slot, edge],
            recv_sem=final_recv.at[slot],
            device_id=where,
            device_id_type=MESH,
        )

    def crossing_copy(batch):
        return final_copy(leaving.at[batch], batches + batch, 0, {"section": entry, "group": 0})

    def all_bytes(ref, sem):
        return pltpu.make_async_copy(ref, ref, sem)

    def stage_a(batch):
        all_bytes(stream.at[batch], stream_recv.at[batch]).wait()
        values = stream[batch].astype(jnp.float32)
        squares = jnp.sum(values * values, axis=1, keepdims=True)
        scaled = (values * gain_ref[...]).astype(jnp.bfloat16)
        mixed = jnp.dot(scaled, win_ref[...], preferred_element_type=jnp.float32)
        squares = jnp.broadcast_to(squares, (ROWS, LANES))
        coarse = squares.astype(jnp.bfloat16).astype(jnp.float32)
        fine = squares - coarse
        for half in range(2):
            rows = slice(half * HALF, (half + 1) * HALF)
            partial[batch, half, :, :units] = jnp.concatenate(
                [mixed[rows, :units], mixed[rows, units:]], 0
            ).astype(jnp.bfloat16)
            partial[batch, half, :, units:] = jnp.concatenate(
                [coarse[rows], fine[rows]], 0
            ).astype(jnp.bfloat16)
        for offset in range(1, tensor_count):
            piece_copy(batch, offset).start()

    def stage_b(batch):
        all_bytes(pieces.at[batch], piece_recv.at[batch]).wait()
        total = partial[batch, core].astype(jnp.float32)
        for offset in range(1, tensor_count):
            total += pieces[batch, offset - 1].astype(jnp.float32)
        squares = total[:HALF, units:units + 1] + total[HALF:, units:units + 1]
        scale = lax.rsqrt(squares / (width * tensor_count) + epsilon)
        gate = total[:HALF, :units] * scale
        up = total[HALF:, :units] * scale
        mine[batch] = gate / (1.0 + jnp.exp(-gate)) * up
        twin_copy(batch).start()

    def stage_c(batch):
        twin_copy(batch).wait_recv()
        here, there = mine[batch], twin_rows[batch]
        hidden = jnp.concatenate(
            [jnp.where(core == 0, here, there), jnp.where(core == 0, there, here)], 0
        ).astype(jnp.bfloat16)
        update = jnp.dot(hidden, wout_ref[...], preferred_element_type=jnp.float32)
        leaving[batch] = (stream[batch].astype(jnp.float32) + update).astype(jnp.bfloat16)

        @pl.when(jnp.logical_not(last_section))
        def _():
            stream_copy(batch).start()

        @pl.when(jnp.logical_and(last_section, in_first))
        def _():
            final[batch] = leaving[batch]
            for edge, (_, target) in enumerate(edges_a):
                final_copy(leaving.at[batch], batch, edge, {"section": target}).start()

        @pl.when(crossing_out)
        def _():
            crossing_copy(batch).start()

    def relay():
        loads[0].wait()
        loads[1].wait()

        def step(index, carry):
            @pl.when(index < batches)
            def _():
                stage_a(index)

            @pl.when(index >= 1)
            def _():
                stage_b(index - 1)
                stage_c(index - 1)

            return carry

        lax.fori_loop(0, batches + 1, step, 0)

    def pass_on(slot, edges, root):
        @pl.when(jnp.logical_not(root))
        def _():
            all_bytes(final.at[slot], final_recv.at[slot]).wait()

            @pl.when(in_first)
            def _():
                for edge, (sends, target) in enumerate(edges):
                    @pl.when(sends)
                    def _(edge=edge, target=target):
                        final_copy(final.at[slot], slot, edge, {"section": target}).start()

    def logit_copy(chunk, offset):
        target = (tensor + offset) % tensor_count
        return pltpu.make_async_remote_copy(
            src_ref=logit_out.at[chunk, target],
            dst_ref=logit_in.at[chunk, offset - 1],
            send_sem=logit_send.at[chunk],
            recv_sem=logit_recv.at[chunk],
            device_id={"tensor": target},
            device_id_type=MESH,
        )

    def pol_copy(chunk):
        return pltpu.make_async_remote_copy(
            src_ref=pol_out.at[chunk],
            dst_ref=pol_in.at[chunk],
            send_sem=pol_send.at[chunk],
            recv_sem=pol_recv.at[chunk],
            device_id={"group": 1 - group},
            device_id_type=MESH,
        )

    per_chunk = CHUNK // ROWS

    def head_product(chunk):
        rows = jnp.concatenate(
            [
                final[pl.ds(chunk * per_chunk, per_chunk)].reshape(CHUNK, width),
                final[pl.ds(batches + chunk * per_chunk, per_chunk)].reshape(CHUNK, width),
            ],
            0,
        )
        logits = lax.dot_general(
            rows, head_ref[...], (((1,), (1,)), ((), ())), preferred_element_type=jnp.float32
        )
        logit_out[chunk] = logits.astype(jnp.bfloat16).reshape(
            tensor_count, 2 * CHUNK // tensor_count, vocab_block
        )
        for offset in range(1, tensor_count):
            logit_copy(chunk, offset).start()

    def head_total(chunk):
        all_bytes(logit_in.at[chunk], logit_recv.at[chunk]).wait()
        total = logit_out[chunk, tensor].astype(jnp.float32)
        for offset in range(1, tensor_count):
            total += logit_in[chunk, offset - 1].astype(jnp.float32)

        @pl.when(in_second)
        def _():
            pol_out[chunk] = total
            pol_copy(chunk).start()

        @pl.when(in_first)
        def _():
            pol_copy(chunk).wait_recv()
            pol = pol_in[chunk]
            rows = pl.ds(pl.multiple_of(chunk * BLOCK, BLOCK), BLOCK)
            ids = section * vocab_block + lax.broadcasted_iota(jnp.int32, pol.shape, 1)
            picked = jnp.where(ids == wanted_ref[rows, :1], pol, 0.0)
            peak_pol = jnp.max(pol, axis=1, keepdims=True)
            peak_ref = jnp.max(total, axis=1, keepdims=True)
            weights_pol = jnp.exp(pol - peak_pol)
            weights_ref = jnp.exp(total - peak_ref)
            stats = [
                peak_pol,
                peak_ref,
                jnp.sum(weights_pol, axis=1, keepdims=True),
                jnp.sum(weights_ref, axis=1, keepdims=True),
                jnp.sum(weights_pol * (pol - total), axis=1, keepdims=True),
                jnp.sum(picked, axis=1, keepdims=True),
            ]
            lane = lax.broadcasted_iota(jnp.int32, (BLOCK, LANES), 1)
            block = jnp.zeros((BLOCK, LANES), jnp.float32)
            for index, stat in enumerate(stats):
                block = jnp.where(lane == index, stat, block)
            stat_rows[rows, :] = block

    def head_work():
        loads[2].wait()

        def step(index, carry):
            @pl.when(jnp.logical_and(index >= lag_a, index < batches + lag_a))
            def _():
                pass_on(index - lag_a, edges_a, jnp.logical_and(last_section, in_first))

            @pl.when(jnp.logical_and(index >= lag_b, index < batches + lag_b))
            def _():
                pass_on(batches + index - lag_b, edges_b, jnp.bool_(False))

            done = index - lag_most + 1
            chunk = done // per_chunk - 1
            full = jnp.logical_and(done > 0, done % per_chunk == 0)

            @pl.when(jnp.logical_and(full, chunk < chunks))
            def _():
                head_product(chunk)

            @pl.when(jnp.logical_and(full, jnp.logical_and(chunk >= 1, chunk <= chunks)))
            def _():
                head_total(chunk - 1)

            return carry

        lax.fori_loop(0, batches + lag_limit + per_chunk, step, 0)

    def stat_copy(to_section, to_group):
        return pltpu.make_async_remote_copy(
            src_ref=stat_out,
            dst_ref=stat_in.at[section],
            send_sem=stat_send,
            recv_sem=stat_recv,
            device_id={"section": to_section, "group": to_group},
            device_id_type=MESH,
        )

    @pl.when(jnp.logical_and(in_first, late_half))
    def _():
        send_policy()

    head_phase = jnp.where(jnp.logical_and(in_second, late_half), 0, 2)

    def phase(index, carry):
        @pl.when(index == 1)
        def _():
            relay()

        @pl.when(jnp.logical_and(index == 2, jnp.logical_and(in_first, jnp.logical_not(late_half))))
        def _():
            send_policy()

        @pl.when(index == head_phase)
        def _():
            head_work()

        return carry

    lax.fori_loop(0, 3, phase, 0)

    @pl.when(in_first)
    def _():
        block = jnp.transpose(stat_rows[...])[:8]
        stat_out[...] = block
        stat_in[section] = block
        for offset in range(section_count):
            to_section = (section + offset) % section_count
            if offset:
                stat_copy(to_section, 0).start()
            stat_copy(to_section, 1).start()

    def drain(batch, carry):
        all_bytes(pieces.at[batch], piece_send.at[batch]).wait()
        twin_copy(batch).wait_send()

        @pl.when(jnp.logical_not(last_section))
        def _():
            stream_copy(batch).wait_send()

        @pl.when(in_first)
        def _():
            for first, edges in ((0, edges_a), (batches, edges_b)):
                for edge, (sends, target) in enumerate(edges):
                    @pl.when(sends)
                    def _(edge=edge, target=target, slot=first + batch):
                        final_copy(final.at[slot], slot, edge, {"section": target}).wait_send()

            for place in range(PER):
                policy_copy(batch * PER + place).wait_send()

        @pl.when(crossing_out)
        def _():
            crossing_copy(batch).wait_send()

        return carry

    lax.fori_loop(0, batches, drain, 0)

    def drain_logits(chunk, carry):
        all_bytes(logit_in.at[chunk], logit_send.at[chunk]).wait()

        @pl.when(in_second)
        def _():
            pol_copy(chunk).wait_send()

        return carry

    lax.fori_loop(0, chunks, drain_logits, 0)

    @pl.when(in_first)
    def _():
        all_bytes(stat_in.at[pl.ds(0, section_count - 1)], stat_recv).wait()

    @pl.when(in_second)
    def _():
        all_bytes(stat_in.at[pl.ds(0, section_count)], stat_recv).wait()

    peaks_pol = [stat_in[index, 0:1] for index in range(section_count)]
    peaks_ref = [stat_in[index, 1:2] for index in range(section_count)]
    peak_pol, peak_ref = peaks_pol[0], peaks_ref[0]
    for index in range(1, section_count):
        peak_pol = jnp.maximum(peak_pol, peaks_pol[index])
        peak_ref = jnp.maximum(peak_ref, peaks_ref[index])
    total_pol = jnp.zeros_like(peak_pol)
    total_ref = jnp.zeros_like(peak_pol)
    cross = jnp.zeros_like(peak_pol)
    chosen = jnp.zeros_like(peak_pol)
    for index in range(section_count):
        shift_pol = jnp.exp(peaks_pol[index] - peak_pol)
        shift_ref = jnp.exp(peaks_ref[index] - peak_ref)
        total_pol += shift_pol * stat_in[index, 2:3]
        total_ref += shift_ref * stat_in[index, 3:4]
        cross += shift_pol * stat_in[index, 4:5]
        chosen += stat_in[index, 5:6]
    lse_pol = peak_pol + jnp.log(total_pol)
    lse_ref = peak_ref + jnp.log(total_ref)
    out_ref[0:1] = cross / total_pol - lse_pol + lse_ref
    out_ref[1:2] = chosen - lse_pol
    out_ref[2:] = jnp.zeros((6, LANES), jnp.float32)

    @pl.when(in_first)
    def _():
        all_bytes(stat_in.at[pl.ds(0, 2 * section_count - 1)], stat_send).wait()


def token_terms(rows, gain, weight_in, weight_out, policy_rows, head, wanted):
    tensor_count = lax.axis_size("tensor")
    section_count = lax.axis_size("section")
    blocks, _, width = rows.shape
    batches = blocks // PER
    units = weight_out.shape[0]
    vocab_block = head.shape[0]
    chunks = blocks * BLOCK // CHUNK
    piece = (ROWS, units + LANES)
    logit = (BLOCK, vocab_block)
    dma = pltpu.SemaphoreType.DMA
    vmem = pl.BlockSpec(memory_space=pltpu.VMEM)
    hbm = pl.BlockSpec(memory_space=pl.ANY)
    bf16, f32 = jnp.bfloat16, jnp.float32
    return pl.pallas_call(
        kernel,
        out_shape=jax.ShapeDtypeStruct((8, LANES), f32),
        in_specs=[hbm, vmem, hbm, hbm, hbm, hbm, vmem],
        out_specs=vmem,
        scratch_shapes=[
            pltpu.VMEM(weight_in.shape, bf16),
            pltpu.VMEM(weight_out.shape, bf16),
            pltpu.VMEM(head.shape, bf16),
            pltpu.VMEM((batches, ROWS, width), bf16),
            pltpu.VMEM((batches, 2) + piece, bf16),
            pltpu.VMEM((batches, tensor_count - 1) + piece, bf16),
            pltpu.VMEM((batches, HALF, units), f32),
            pltpu.VMEM((batches, HALF, units), f32),
            pltpu.VMEM((batches, ROWS, width), bf16),
            pltpu.VMEM((2 * batches, ROWS, width), bf16),
            pltpu.VMEM((chunks, tensor_count) + logit, bf16),
            pltpu.VMEM((chunks, tensor_count - 1) + logit, bf16),
            pltpu.VMEM((chunks,) + logit, f32),
            pltpu.VMEM((chunks,) + logit, f32),
            pltpu.VMEM((LANES, LANES), f32),
            pltpu.VMEM((8, LANES), f32),
            pltpu.VMEM((2 * section_count, 8, LANES), f32),
            dma((3,)),
            dma((batches,)),
            dma((batches,)),
            dma((batches,)),
            dma((batches,)),
            dma((batches,)),
            dma((batches,)),
            dma((2 * batches, 3)),
            dma((2 * batches,)),
            dma((blocks,)),
            dma((chunks,)),
            dma((chunks,)),
            dma((chunks,)),
            dma((chunks,)),
            dma,
            dma,
        ],
        compiler_params=pltpu.CompilerParams(
            collective_id=0, has_side_effects=True, vmem_limit_bytes=48 * 1024 * 1024
        ),
        name="token_terms",
    )(rows, gain, weight_in, weight_out, policy_rows, head, wanted)


def advantages(rewards, prompt_ids):
    same = (prompt_ids[:, None] == prompt_ids[None, :]).astype(jnp.float32)
    counts = jnp.sum(same, axis=1)
    means = jnp.sum(same * rewards[None, :], axis=1) / counts
    spread = rewards[None, :] - means[:, None]
    variance = jnp.sum(same * spread * spread, axis=1) / counts
    return (rewards - means) / jnp.maximum(jnp.sqrt(variance), 1.0)


def shards(
    ref_input, norm_gain, w_in, w_out, policy_hidden, heads, sampled, live_mask, rewards, prompt_ids
):
    tensor_here = lax.axis_index("tensor")
    group_count = lax.axis_size("group")
    group_here = lax.axis_index("group")
    tokens = sampled.shape[0]
    per_tensor = tokens // lax.axis_size("tensor")
    local_rows = per_tensor // group_count
    width = ref_input.shape[3]
    wanted = lax.dynamic_slice_in_dim(sampled, tensor_here * per_tensor, per_tensor, 0)
    terms = token_terms(
        ref_input.reshape(-1, BLOCK, width),
        norm_gain,
        w_in[0],
        w_out[0],
        policy_hidden.reshape(-1, BLOCK, width),
        heads[0],
        jnp.broadcast_to(wanted[:, None], (per_tensor, LANES)),
    )
    terms = lax.dynamic_slice_in_dim(terms[:2], group_here * local_rows, local_rows, 1)
    token_kl, log_prob = terms[0], terms[1]
    row_start = (tensor_here * group_count + group_here) * local_rows
    token_adv = lax.dynamic_slice_in_dim(
        jnp.repeat(advantages(rewards, prompt_ids), RLEN), row_start, local_rows, 0
    )
    live = lax.dynamic_slice_in_dim(live_mask, row_start, local_rows, 0).astype(jnp.float32)
    token_loss = live * (penalty * token_kl - token_adv * log_prob) / RLEN
    return (token_kl, token_loss)


def solution(mesh):
    in_specs = (
        P("group", None, None, "tensor"),
        P("section", "tensor"),
        P("section", "tensor", None),
        P("section", None, "tensor"),
        P("group", "tensor"),
        P("group", "section", "tensor"),
        P(),
        P(),
        P(),
        P(),
    )
    out_specs = (P(("tensor", "group")), P(("tensor", "group")))
    return jax.shard_map(shards, mesh=mesh, in_specs=in_specs, out_specs=out_specs, check_vma=False)
```

time: 723 us -> 325 us (0.45); the launches traced: 712 us -> 325 us
  Pallas kernels: 478 us -> 317 us
  waiting for transfers between devices: 152 us -> 0 us
  blocking collectives: 34.3 us -> 0 us
  starting transfers between devices: 16.1 us -> 0 us
  between operations: 14.1 us -> 0.68 us
    pallas_call x1, Pallas kernels: 478 us -> 317 us  [token_terms(): pl.pallas_call(kernel, out_shape=jax.ShapeDtypeStruct((8, LANES), f32), i...]
    reduce_scatter x1 -> x0, waiting for transfers between devices: 145 us -> none  [shards(): lax.psum_scatter(lax.dot_general(hidden_rows, heads[0], (((1,), (1,)), ((...]
    all_gather x1 -> x0, blocking collectives: 34.3 us -> none  [shards(): stats = lax.all_gather(stats, 'section')]
    ppermute x1 -> x0, starting transfers between devices: 9.71 us -> none  [shards(): policy_other = lax.ppermute(policy_hidden, 'group', [(0, 1)])]
  transfers between devices with their start and end apart: 3 -> 0, of which waited for: 2 -> 0; matrix products, arithmetic and copies ran while one was open for 0% -> 0% of each run, Pallas kernels for 67% -> 0%
where the time goes in v2:
time: 325 us
  Pallas kernels  317 us (98%)
  local copies, waits for them, and re-layouts  5.62 us (2%)
    pallas_call x1, Pallas kernels, token_terms(): pl.pallas_call(kernel, out_shape=jax.ShapeDtypeStruct((8, LANES), f32), i...  317 us

profile of v2, /device:TPU:1, one launch (start us, length us, event | category | flops | bytes accessed | tf_op | source)
XLA Modules:
  0.0 324.7 jit_solution(2604733809810054807)
XLA Ops:
  0.6 0.8 dynamic_slice.12
  1.4 0.1 broadcast_in_dim.4.wanted_ref
  1.5 0.0 copy-start
  1.5 1.4 copy-done
  2.9 0.0 copy-start.1
  2.9 1.2 copy-done.1
  4.1 0.0 copy-start.2
  4.1 1.2 copy-done.2
  5.3 0.0 copy-start.3
  5.3 0.7 copy-done.3
  6.0 0.0 copy-start.4
  6.0 0.0 copy-start.5
  6.0 316.7 %token_terms.1 = f32[8,128]{1,0:T(8,128)S(1)} custom-call(bf16[16,16,2048]{2,1,0:T(8,128)(2,1)S(1)} %bitcast.17, f32[1,2048]{1,0:T(1,128)S(1)} %copy-done.3, bf16[2048,768]{1,0:T(8,128)(2,1)} %bitcast.20, bf16[384,2048]{1,0:T(8,128)(2,1)S(1)} %bitcast.16, bf16[16,16,2048]{2,1,0:T(8,128)(2,1)S(1)} %bitcast.18, bf16[1024,2048]{1,0:T(8,128)(2,1)} %bitcast.19, ...), custom_call_target="tpu_custom_call" | custom-call | tf_op jit(solution)/shard_map/token_terms/pallas_call | solution.py:545
  322.8 0.1 constant_dynamic-slice_fusion
  322.9 0.0 copy-done.4
  322.9 0.0 copy-done.5
  322.9 0.2 fusion.3
  323.1 0.2 fusion.1
  323.3 0.1 broadcast_in_dim.5
  323.4 0.1 reshape.24
  323.4 1.3 fusion.6
  (3 shorter events, 0.0 us)
Async XLA Ops:
  1.5 1.4 copy-start
  2.9 1.2 copy-start.1
  4.1 1.2 copy-start.2
  5.3 0.7 copy-start.3
  6.0 316.9 %copy-start.4 = (s32[8]{0:T(128)S(1)}, s32[8]{0:T(128)}, u32[]{:S(2)}) copy-start(s32[8]{0:T(128)} %param.19) | copy-start | bytes 100
  6.0 316.9 %copy-start.5 = (f32[8]{0:T(128)S(1)}, f32[8]{0:T(128)}, u32[]{:S(2)}) copy-start(f32[8]{0:T(128)} %param.18) | copy-start | bytes 100

commit v3 on v2

--- a/solution.py
+++ b/solution.py
@@ -87,6 +87,9 @@
     lag_most = jnp.maximum(lag_a, lag_b)
     lag_limit = 6
     crossing_out = jnp.logical_and(last_section, in_second)
+    policy_source = jnp.logical_and(in_first, late_half)
+    policy_passes = jnp.logical_and(in_second, late_half)
+    across = (SIDE - 1 - section // SIDE) * SIDE + section % SIDE
 
     loads = [
         pltpu.make_async_copy(win_hbm, win_ref, load_sem.at[0]),
@@ -143,6 +146,10 @@
         for offset in range(1, section_count):
             greet({"section": (section + offset) % section_count})
 
+    @pl.when(in_second)
+    def _():
+        greet({"section": across})
+
     @pl.when(jnp.logical_and(in_second, jnp.logical_not(first_section)))
     def _():
         greet({"section": section - 1})
@@ -154,7 +161,7 @@
     neighbours = as_count(jnp.logical_not(first_section)) + as_count(jnp.logical_not(last_section))
     pl.semaphore_wait(
         barrier,
-        tensor_count - 1 + section_count + jnp.where(in_first, section_count - 1, neighbours),
+        tensor_count - 1 + section_count + jnp.where(in_first, section_count - 1, neighbours + 1),
     )
 
     def policy_copy(place):
@@ -305,6 +312,10 @@
                     @pl.when(sends)
                     def _(edge=edge, target=target):
                         final_copy(final.at[slot], slot, edge, {"section": target}).start()
+
+            @pl.when(jnp.logical_and(policy_passes, slot < batches))
+            def _():
+                final_copy(final.at[slot], slot, 0, {"section": across}).start()
 
     def logit_copy(chunk, offset):
         target = (tensor + offset) % tensor_count
@@ -420,20 +431,16 @@
             device_id_type=MESH,
         )
 
-    @pl.when(jnp.logical_and(in_first, late_half))
+    @pl.when(policy_source)
     def _():
         send_policy()
 
-    head_phase = jnp.where(jnp.logical_and(in_second, late_half), 0, 2)
+    head_phase = jnp.where(policy_passes, 0, 2)
 
     def phase(index, carry):
         @pl.when(index == 1)
         def _():
             relay()
-
-        @pl.when(jnp.logical_and(index == 2, jnp.logical_and(in_first, jnp.logical_not(late_half))))
-        def _():
-            send_policy()
 
         @pl.when(index == head_phase)
         def _():
@@ -470,8 +477,14 @@
                     def _(edge=edge, target=target, slot=first + batch):
                         final_copy(final.at[slot], slot, edge, {"section": target}).wait_send()
 
+        @pl.when(policy_source)
+        def _():
             for place in range(PER):
                 policy_copy(batch * PER + place).wait_send()
+
+        @pl.when(policy_passes)
+        def _():
+            final_copy(final.at[batch], batch, 0, {"section": across}).wait_send()
 
         @pl.when(crossing_out)
         def _():
@@ -540,7 +553,7 @@
     logit = (BLOCK, vocab_block)
     dma = pltpu.SemaphoreType.DMA
     vmem = pl.BlockSpec(memory_space=pltpu.VMEM)
-    hbm = pl.BlockSpec(memory_space=pl.ANY)
+    hbm = pl.BlockSpec(memory_space=pltpu.HBM)
     bf16, f32 = jnp.bfloat16, jnp.float32
     return pl.pallas_call(
         kernel,

time: 325 us -> 284 us (0.87)
  Pallas kernels: 317 us -> 276 us
    pallas_call x1, Pallas kernels: 317 us -> 276 us  [token_terms(): pl.pallas_call(kernel, out_shape=jax.ShapeDtypeStruct((8, LANES), f32), i...]
where the time goes in v3:
time: 284 us
  Pallas kernels  276 us (97%)
  local copies, waits for them, and re-layouts  5.62 us (2%)
    pallas_call x1, Pallas kernels, token_terms(): pl.pallas_call(kernel, out_shape=jax.ShapeDtypeStruct((8, LANES), f32), i...  276 us

profile of v3, /device:TPU:1, one launch (start us, length us, event | category | flops | bytes accessed | tf_op | source)
XLA Modules:
  0.0 284.0 jit_solution(10801002989393405764)
XLA Ops:
  0.6 0.8 dynamic_slice.12
  1.4 0.1 broadcast_in_dim.4.wanted_ref
  1.5 0.0 copy-start
  1.5 1.4 copy-done
  2.9 0.0 copy-start.1
  2.9 1.2 copy-done.1
  4.1 0.0 copy-start.2
  4.1 1.2 copy-done.2
  5.3 0.0 copy-start.3
  5.3 0.7 copy-done.3
  6.0 0.0 copy-start.4
  6.0 0.0 copy-start.5
  6.0 276.0 %token_terms.1 = f32[8,128]{1,0:T(8,128)S(1)} custom-call(bf16[16,16,2048]{2,1,0:T(8,128)(2,1)S(1)} %bitcast.17, f32[1,2048]{1,0:T(1,128)S(1)} %copy-done.3, bf16[2048,768]{1,0:T(8,128)(2,1)} %bitcast.20, bf16[384,2048]{1,0:T(8,128)(2,1)S(1)} %bitcast.16, bf16[16,16,2048]{2,1,0:T(8,128)(2,1)S(1)} %bitcast.18, bf16[1024,2048]{1,0:T(8,128)(2,1)} %bitcast.19, ...), custom_call_target="tpu_custom_call" | custom-call | tf_op jit(solution)/shard_map/token_terms/pallas_call | solution.py:558
  282.1 0.1 constant_dynamic-slice_fusion
  282.1 0.0 copy-done.4
  282.1 0.0 copy-done.5
  282.1 0.2 fusion.3
  282.3 0.2 fusion.1
  282.5 0.1 broadcast_in_dim.5
  282.6 0.1 reshape.24
  282.7 1.3 fusion.6
  (3 shorter events, 0.0 us)
Async XLA Ops:
  1.5 1.4 copy-start
  2.9 1.2 copy-start.1
  4.1 1.2 copy-start.2
  5.3 0.7 copy-start.3
  6.0 276.1 %copy-start.4 = (s32[8]{0:T(128)S(1)}, s32[8]{0:T(128)}, u32[]{:S(2)}) copy-start(s32[8]{0:T(128)} %param.19) | copy-start | bytes 100
  6.0 276.1 %copy-start.5 = (f32[8]{0:T(128)S(1)}, f32[8]{0:T(128)}, u32[]{:S(2)}) copy-start(f32[8]{0:T(128)} %param.18) | copy-start | bytes 100

commit v4 on v3

--- a/solution.py
+++ b/solution.py
@@ -53,11 +53,14 @@
 
 
 def kernel(
-    x_ref, gain_ref, win_hbm, wout_hbm, policy_ref, head_hbm, wanted_ref, out_ref,
-    win_ref, wout_ref, head_ref,
-    stream, partial, pieces, mine, twin_rows, leaving, final,
+    x_ref, gain_hbm, win_hbm, wout_hbm, policy_ref, head_hbm, sampled_hbm, out_ref,
+    gain_ref, win_ref, wout_ref, before_ref, head_ref, sampled_ref,
+    blend_out, blend_in, blend,
+    stream, partial, pieces, square_out, square_in, mine, arrived, twin_rows, leaving, ending, final,
     logit_out, logit_in, pol_out, pol_in, stat_rows, stat_out, stat_in,
-    load_sem, piece_send, piece_recv, twin_send, twin_recv, stream_send, stream_recv,
+    load_sem, weight_send, weight_recv, blend_send, blend_recv,
+    piece_send, piece_recv, square_send, square_recv, unit_send, unit_recv,
+    twin_send, twin_recv, stream_send, stream_recv,
     final_send, final_recv, policy_send, logit_send, logit_recv, pol_send, pol_recv,
     stat_send, stat_recv,
 ):
@@ -92,9 +95,11 @@
     across = (SIDE - 1 - section // SIDE) * SIDE + section % SIDE
 
     loads = [
-        pltpu.make_async_copy(win_hbm, win_ref, load_sem.at[0]),
-        pltpu.make_async_copy(wout_hbm, wout_ref, load_sem.at[1]),
-        pltpu.make_async_copy(head_hbm, head_ref, load_sem.at[2]),
+        pltpu.make_async_copy(gain_hbm, gain_ref, load_sem.at[0]),
+        pltpu.make_async_copy(win_hbm, win_ref, load_sem.at[1]),
+        pltpu.make_async_copy(wout_hbm, wout_ref, load_sem.at[2]),
+        pltpu.make_async_copy(head_hbm, head_ref, load_sem.at[3]),
+        pltpu.make_async_copy(sampled_hbm, sampled_ref, load_sem.at[4]),
     ]
 
     def own_block(source, target, place, sem):
@@ -106,7 +111,7 @@
 
     places = batches * PER
 
-    @pl.when(first_section)
+    @pl.when(section < 2)
     def _():
         def fetch(place, carry):
             own_block(x_ref, stream, place, stream_recv).start()
@@ -129,8 +134,6 @@
 
         lax.fori_loop(0, places, fetch, 0)
 
-    stat_rows[...] = jnp.zeros_like(stat_rows)
-
     barrier = pltpu.get_barrier_semaphore()
 
     def greet(where):
@@ -158,11 +161,45 @@
     def _():
         greet({"section": section + 1})
 
+    @pl.when(jnp.logical_not(first_section))
+    def _():
+        greet({"section": section - 1, "tensor": twin})
+
+    @pl.when(jnp.logical_not(last_section))
+    def _():
+        greet({"section": section + 1, "tensor": twin})
+
     neighbours = as_count(jnp.logical_not(first_section)) + as_count(jnp.logical_not(last_section))
     pl.semaphore_wait(
         barrier,
-        tensor_count - 1 + section_count + jnp.where(in_first, section_count - 1, neighbours + 1),
+        tensor_count - 1 + section_count + neighbours + jnp.where(in_first, section_count - 1, neighbours + 1),
     )
+
+    def all_bytes(ref, sem):
+        return pltpu.make_async_copy(ref, ref, sem)
+
+    def to_peer(source, target, send_sem, recv_sem, offset):
+        return pltpu.make_async_remote_copy(
+            src_ref=source,
+            dst_ref=target,
+            send_sem=send_sem,
+            recv_sem=recv_sem,
+            device_id={"tensor": (tensor + offset) % tensor_count},
+            device_id_type=MESH,
+        )
+
+    weight_copy = pltpu.make_async_remote_copy(
+        src_ref=wout_hbm,
+        dst_ref=before_ref,
+        send_sem=weight_send,
+        recv_sem=weight_recv,
+        device_id={"section": section + 1},
+        device_id_type=MESH,
+    )
+
+    @pl.when(jnp.logical_not(last_section))
+    def _():
+        weight_copy.start()
 
     def policy_copy(place):
         return pltpu.make_async_remote_copy(
@@ -181,14 +218,13 @@
 
         lax.fori_loop(0, places, one, 0)
 
-    def piece_copy(batch, offset):
-        target = (tensor + offset) % tensor_count
+    def unit_copy(batch, where):
         return pltpu.make_async_remote_copy(
-            src_ref=partial.at[batch, target % 2],
-            dst_ref=pieces.at[batch, offset - 1],
-            send_sem=piece_send.at[batch],
-            recv_sem=piece_recv.at[batch],
-            device_id={"tensor": target},
+            src_ref=mine.at[batch],
+            dst_ref=arrived.at[batch, core],
+            send_sem=unit_send.at[batch],
+            recv_sem=unit_recv.at[batch, core],
+            device_id={"section": section + 1, "tensor": where},
             device_id_type=MESH,
         )
 
@@ -223,69 +259,138 @@
         )
 
     def crossing_copy(batch):
-        return final_copy(leaving.at[batch], batches + batch, 0, {"section": entry, "group": 0})
-
-    def all_bytes(ref, sem):
-        return pltpu.make_async_copy(ref, ref, sem)
+        return final_copy(ending.at[batch], batches + batch, 0, {"section": entry, "group": 0})
+
+    def set_up():
+        loads[0].wait()
+        loads[1].wait()
+
+        @pl.when(first_section)
+        def _():
+            before_ref[...] = jnp.zeros_like(before_ref)
+            blend[...] = jnp.zeros_like(blend)
+            arrived[...] = jnp.zeros_like(arrived)
+
+        @pl.when(jnp.logical_not(first_section))
+        def _():
+            all_bytes(before_ref, weight_recv).wait()
+            share = units // tensor_count
+
+            def product(pair, carry):
+                rows = pl.ds(pl.multiple_of(pair * 2 * share, 2 * share), 2 * share)
+                scaled = (before_ref[rows].astype(jnp.float32) * gain_ref[...]).astype(jnp.bfloat16)
+                out = jnp.dot(scaled, win_ref[...], preferred_element_type=jnp.float32)
+                blend_out[pl.ds(pair * 2, 2)] = out.astype(jnp.bfloat16).reshape(2, share, 2 * units)
+                return carry
+
+            lax.fori_loop(0, tensor_count // 2, product, 0)
+            for offset in range(1, tensor_count):
+                to_peer(
+                    blend_out.at[(tensor + offset) % tensor_count], blend_in.at[offset - 1],
+                    blend_send.at[0], blend_recv.at[0], offset,
+                ).start()
+            all_bytes(blend_in, blend_recv.at[0]).wait()
+            total = blend_out[tensor].astype(jnp.float32)
+            for offset in range(1, tensor_count):
+                total += blend_in[offset - 1].astype(jnp.float32)
+            blend[tensor] = total.astype(jnp.bfloat16)
+            for offset in range(1, tensor_count):
+                to_peer(
+                    blend.at[tensor], blend.at[tensor], blend_send.at[1], blend_recv.at[1], offset
+                ).start()
 
     def stage_a(batch):
         all_bytes(stream.at[batch], stream_recv.at[batch]).wait()
-        values = stream[batch].astype(jnp.float32)
-        squares = jnp.sum(values * values, axis=1, keepdims=True)
-        scaled = (values * gain_ref[...]).astype(jnp.bfloat16)
+        scaled = (stream[batch].astype(jnp.float32) * gain_ref[...]).astype(jnp.bfloat16)
         mixed = jnp.dot(scaled, win_ref[...], preferred_element_type=jnp.float32)
-        squares = jnp.broadcast_to(squares, (ROWS, LANES))
-        coarse = squares.astype(jnp.bfloat16).astype(jnp.float32)
-        fine = squares - coarse
         for half in range(2):
             rows = slice(half * HALF, (half + 1) * HALF)
-            partial[batch, half, :, :units] = jnp.concatenate(
+            partial[batch, half] = jnp.concatenate(
                 [mixed[rows, :units], mixed[rows, units:]], 0
             ).astype(jnp.bfloat16)
-            partial[batch, half, :, units:] = jnp.concatenate(
-                [coarse[rows], fine[rows]], 0
-            ).astype(jnp.bfloat16)
         for offset in range(1, tensor_count):
-            piece_copy(batch, offset).start()
+            to_peer(
+                partial.at[batch, (tensor + offset) % 2], pieces.at[batch, offset - 1],
+                piece_send.at[batch], piece_recv.at[batch], offset,
+            ).start()
+
+    def stage_c(batch):
+        @pl.when(jnp.logical_not(first_section))
+        def _():
+            for half in range(2):
+                all_bytes(arrived.at[batch, half], unit_recv.at[batch, half]).wait()
+
+        hidden = jnp.concatenate([arrived[batch, 0], arrived[batch, 1]], 0)
+        update = jnp.dot(hidden, before_ref[...], preferred_element_type=jnp.float32)
+        fresh = (stream[batch].astype(jnp.float32) + update).astype(jnp.bfloat16)
+        leaving[batch] = fresh
+
+        @pl.when(jnp.logical_and(section > 0, jnp.logical_not(last_section)))
+        def _():
+            stream_copy(batch).start()
+
+        values = fresh.astype(jnp.float32)
+        squares = jnp.broadcast_to(jnp.sum(values * values, axis=1, keepdims=True), (ROWS, LANES))
+        square_out[batch] = squares.reshape(2, HALF, LANES)
+        for offset in range(1, tensor_count):
+            to_peer(
+                square_out.at[batch, (tensor + offset) % 2], square_in.at[batch, offset - 1],
+                square_send.at[batch], square_recv.at[batch], offset,
+            ).start()
 
     def stage_b(batch):
+        @pl.when(jnp.logical_and(batch == 0, jnp.logical_not(first_section)))
+        def _():
+            all_bytes(blend.at[pl.ds(0, tensor_count - 1)], blend_recv.at[1]).wait()
+
+        ahead = jnp.dot(
+            arrived[batch, core],
+            blend[...].reshape(units, 2 * units),
+            preferred_element_type=jnp.float32,
+        )
         all_bytes(pieces.at[batch], piece_recv.at[batch]).wait()
         total = partial[batch, core].astype(jnp.float32)
         for offset in range(1, tensor_count):
             total += pieces[batch, offset - 1].astype(jnp.float32)
-        squares = total[:HALF, units:units + 1] + total[HALF:, units:units + 1]
-        scale = lax.rsqrt(squares / (width * tensor_count) + epsilon)
-        gate = total[:HALF, :units] * scale
-        up = total[HALF:, :units] * scale
-        mine[batch] = gate / (1.0 + jnp.exp(-gate)) * up
-        twin_copy(batch).start()
-
-    def stage_c(batch):
+        all_bytes(square_in.at[batch], square_recv.at[batch]).wait()
+        squares = square_out[batch, core]
+        for offset in range(1, tensor_count):
+            squares += square_in[batch, offset - 1]
+        scale = lax.rsqrt(squares[:, :1] / (width * tensor_count) + epsilon)
+        gate = (total[:HALF] + ahead[:, :units]) * scale
+        up = (total[HALF:] + ahead[:, units:]) * scale
+        mine[batch] = (gate / (1.0 + jnp.exp(-gate)) * up).astype(jnp.bfloat16)
+
+        @pl.when(jnp.logical_not(last_section))
+        def _():
+            unit_copy(batch, tensor).start()
+            unit_copy(batch, twin).start()
+
+        @pl.when(last_section)
+        def _():
+            twin_copy(batch).start()
+
+    def stage_d(batch):
         twin_copy(batch).wait_recv()
         here, there = mine[batch], twin_rows[batch]
         hidden = jnp.concatenate(
             [jnp.where(core == 0, here, there), jnp.where(core == 0, there, here)], 0
-        ).astype(jnp.bfloat16)
+        )
         update = jnp.dot(hidden, wout_ref[...], preferred_element_type=jnp.float32)
-        leaving[batch] = (stream[batch].astype(jnp.float32) + update).astype(jnp.bfloat16)
-
-        @pl.when(jnp.logical_not(last_section))
-        def _():
-            stream_copy(batch).start()
-
-        @pl.when(jnp.logical_and(last_section, in_first))
-        def _():
-            final[batch] = leaving[batch]
+        ending[batch] = (leaving[batch].astype(jnp.float32) + update).astype(jnp.bfloat16)
+
+        @pl.when(in_first)
+        def _():
+            final[batch] = ending[batch]
             for edge, (_, target) in enumerate(edges_a):
-                final_copy(leaving.at[batch], batch, edge, {"section": target}).start()
-
-        @pl.when(crossing_out)
+                final_copy(ending.at[batch], batch, edge, {"section": target}).start()
+
+        @pl.when(in_second)
         def _():
             crossing_copy(batch).start()
 
     def relay():
-        loads[0].wait()
-        loads[1].wait()
+        loads[2].wait()
 
         def step(index, carry):
             @pl.when(index < batches)
@@ -295,7 +400,14 @@
             @pl.when(index >= 1)
             def _():
                 stage_b(index - 1)
-                stage_c(index - 1)
+
+            @pl.when(index < batches)
+            def _():
+                stage_c(index)
+
+            @pl.when(jnp.logical_and(index >= 1, last_section))
+            def _():
+                stage_d(index - 1)
 
             return carry
 
@@ -374,7 +486,15 @@
             pol = pol_in[chunk]
             rows = pl.ds(pl.multiple_of(chunk * BLOCK, BLOCK), BLOCK)
             ids = section * vocab_block + lax.broadcasted_iota(jnp.int32, pol.shape, 1)
-            picked = jnp.where(ids == wanted_ref[rows, :1], pol, 0.0)
+            lane = lax.broadcasted_iota(jnp.int32, (BLOCK, LANES), 1)
+            row = lax.broadcasted_iota(jnp.int32, (BLOCK, LANES), 0)
+            first = (tensor % 2) * CHUNK + chunk * BLOCK
+            samples = jnp.broadcast_to(sampled_ref[pl.ds(tensor // 2, 1), :], (BLOCK, LANES))
+            wanted = jnp.sum(
+                jnp.where(lane == first + row, samples.astype(jnp.float32), 0.0),
+                axis=1, keepdims=True,
+            ).astype(jnp.int32)
+            picked = jnp.where(ids == wanted, pol, 0.0)
             peak_pol = jnp.max(pol, axis=1, keepdims=True)
             peak_ref = jnp.max(total, axis=1, keepdims=True)
             weights_pol = jnp.exp(pol - peak_pol)
@@ -387,14 +507,15 @@
                 jnp.sum(weights_pol * (pol - total), axis=1, keepdims=True),
                 jnp.sum(picked, axis=1, keepdims=True),
             ]
-            lane = lax.broadcasted_iota(jnp.int32, (BLOCK, LANES), 1)
             block = jnp.zeros((BLOCK, LANES), jnp.float32)
             for index, stat in enumerate(stats):
                 block = jnp.where(lane == index, stat, block)
             stat_rows[rows, :] = block
 
     def head_work():
-        loads[2].wait()
+        loads[3].wait()
+        loads[4].wait()
+        stat_rows[...] = jnp.zeros_like(stat_rows)
 
         def step(index, carry):
             @pl.when(jnp.logical_and(index >= lag_a, index < batches + lag_a))
@@ -436,6 +557,7 @@
         send_policy()
 
     head_phase = jnp.where(policy_passes, 0, 2)
+    set_up()
 
     def phase(index, carry):
         @pl.when(index == 1)
@@ -463,9 +585,17 @@
 
     def drain(batch, carry):
         all_bytes(pieces.at[batch], piece_send.at[batch]).wait()
-        twin_copy(batch).wait_send()
+        all_bytes(square_in.at[batch], square_send.at[batch]).wait()
 
         @pl.when(jnp.logical_not(last_section))
+        def _():
+            all_bytes(arrived.at[batch], unit_send.at[batch]).wait()
+
+        @pl.when(last_section)
+        def _():
+            twin_copy(batch).wait_send()
+
+        @pl.when(jnp.logical_and(section > 0, jnp.logical_not(last_section)))
         def _():
             stream_copy(batch).wait_send()
 
@@ -491,6 +621,15 @@
             crossing_copy(batch).wait_send()
 
         return carry
+
+    @pl.when(jnp.logical_not(last_section))
+    def _():
+        weight_copy.wait_send()
+
+    @pl.when(jnp.logical_not(first_section))
+    def _():
+        for index in range(2):
+            all_bytes(blend_in, blend_send.at[index]).wait()
 
     lax.fori_loop(0, batches, drain, 0)
 
@@ -541,7 +680,7 @@
         all_bytes(stat_in.at[pl.ds(0, 2 * section_count - 1)], stat_send).wait()
 
 
-def token_terms(rows, gain, weight_in, weight_out, policy_rows, head, wanted):
+def token_terms(rows, gain, weight_in, weight_out, policy_rows, head, sampled):
     tensor_count = lax.axis_size("tensor")
     section_count = lax.axis_size("section")
     blocks, _, width = rows.shape
@@ -549,7 +688,7 @@
     units = weight_out.shape[0]
     vocab_block = head.shape[0]
     chunks = blocks * BLOCK // CHUNK
-    piece = (ROWS, units + LANES)
+    share = units // tensor_count
     logit = (BLOCK, vocab_block)
     dma = pltpu.SemaphoreType.DMA
     vmem = pl.BlockSpec(memory_space=pltpu.VMEM)
@@ -558,17 +697,27 @@
     return pl.pallas_call(
         kernel,
         out_shape=jax.ShapeDtypeStruct((8, LANES), f32),
-        in_specs=[hbm, vmem, hbm, hbm, hbm, hbm, vmem],
+        in_specs=[hbm] * 7,
         out_specs=vmem,
         scratch_shapes=[
+            pltpu.VMEM(gain.shape, f32),
             pltpu.VMEM(weight_in.shape, bf16),
             pltpu.VMEM(weight_out.shape, bf16),
+            pltpu.VMEM(weight_out.shape, bf16),
             pltpu.VMEM(head.shape, bf16),
+            pltpu.VMEM(sampled.shape, jnp.int32),
+            pltpu.VMEM((tensor_count, share, 2 * units), bf16),
+            pltpu.VMEM((tensor_count - 1, share, 2 * units), bf16),
+            pltpu.VMEM((tensor_count, share, 2 * units), bf16),
             pltpu.VMEM((batches, ROWS, width), bf16),
-            pltpu.VMEM((batches, 2) + piece, bf16),
-            pltpu.VMEM((batches, tensor_count - 1) + piece, bf16),
-            pltpu.VMEM((batches, HALF, units), f32),
-            pltpu.VMEM((batches, HALF, units), f32),
+            pltpu.VMEM((batches, 2, ROWS, units), bf16),
+            pltpu.VMEM((batches, tensor_count - 1, ROWS, units), bf16),
+            pltpu.VMEM((batches, 2, HALF, LANES), f32),
+            pltpu.VMEM((batches, tensor_count - 1, HALF, LANES), f32),
+            pltpu.VMEM((batches, HALF, units), bf16),
+            pltpu.VMEM((batches, 2, HALF, units), bf16),
+            pltpu.VMEM((batches, HALF, units), bf16),
+            pltpu.VMEM((batches, ROWS, width), bf16),
             pltpu.VMEM((batches, ROWS, width), bf16),
             pltpu.VMEM((2 * batches, ROWS, width), bf16),
             pltpu.VMEM((chunks, tensor_count) + logit, bf16),
@@ -578,9 +727,17 @@
             pltpu.VMEM((LANES, LANES), f32),
             pltpu.VMEM((8, LANES), f32),
             pltpu.VMEM((2 * section_count, 8, LANES), f32),
-            dma((3,)),
+            dma((5,)),
+            dma,
+            dma,
+            dma((2,)),
+            dma((2,)),
             dma((batches,)),
             dma((batches,)),
+            dma((batches,)),
+            dma((batches,)),
+            dma((batches,)),
+            dma((batches, 2)),
             dma((batches,)),
             dma((batches,)),
             dma((batches,)),
@@ -596,10 +753,10 @@
             dma,
         ],
         compiler_params=pltpu.CompilerParams(
-            collective_id=0, has_side_effects=True, vmem_limit_bytes=48 * 1024 * 1024
+            collective_id=0, has_side_effects=True, vmem_limit_bytes=60 * 1024 * 1024
         ),
         name="token_terms",
-    )(rows, gain, weight_in, weight_out, policy_rows, head, wanted)
+    )(rows, gain, weight_in, weight_out, policy_rows, head, sampled)
 
 
 def advantages(rewards, prompt_ids):
@@ -621,7 +778,6 @@
     per_tensor = tokens // lax.axis_size("tensor")
     local_rows = per_tensor // group_count
     width = ref_input.shape[3]
-    wanted = lax.dynamic_slice_in_dim(sampled, tensor_here * per_tensor, per_tensor, 0)
     terms = token_terms(
         ref_input.reshape(-1, BLOCK, width),
         norm_gain,
@@ -629,7 +785,7 @@
         w_out[0],
         policy_hidden.reshape(-1, BLOCK, width),
         heads[0],
-        jnp.broadcast_to(wanted[:, None], (per_tensor, LANES)),
+        sampled.reshape(-1, LANES),
     )
     terms = lax.dynamic_slice_in_dim(terms[:2], group_here * local_rows, local_rows, 1)
     token_kl, log_prob = terms[0], terms[1]

time: 284 us -> 252 us (0.89)
  Pallas kernels: 276 us -> 249 us
  local copies, waits for them, and re-layouts: 5.62 us -> 0.92 us
    pallas_call x1, Pallas kernels: 276 us -> 249 us  [token_terms(): pl.pallas_call(kernel, out_shape=jax.ShapeDtypeStruct((8, LANES), f32), i...]
    unnamed x12 -> x4, local copies, waits for them, and re-layouts: 4.56 us -> 0.01 us
where the time goes in v4:
time: 252 us
  Pallas kernels  249 us (99%)
    pallas_call x1, Pallas kernels, token_terms(): pl.pallas_call(kernel, out_shape=jax.ShapeDtypeStruct((8, LANES), f32), i...  249 us

profile of v4, /device:TPU:1, one launch (start us, length us, event | category | flops | bytes accessed | tf_op | source)
XLA Modules:
  0.0 252.3 jit_solution(2777256869297375174)
XLA Ops:
  0.6 0.0 copy-start
  0.7 0.0 copy-start.1
  0.7 249.0 %token_terms.1 = f32[8,128]{1,0:T(8,128)} custom-call(bf16[16,16,2048]{2,1,0:T(8,128)(2,1)} %bitcast.20, f32[1,2048]{1,0:T(1,128)} %gain_hbm.1, bf16[2048,768]{1,0:T(8,128)(2,1)} %bitcast.18, bf16[384,2048]{1,0:T(8,128)(2,1)} %bitcast.19, bf16[16,16,2048]{2,1,0:T(8,128)(2,1)} %bitcast.21, bf16[1024,2048]{1,0:T(8,128)(2,1)} %bitcast.17, s32[4,128]{1,0:T(4,128)} %bitcast.22), custom_call_target="tpu_custom_call" | custom-call | tf_op jit(solution)/shard_map/token_terms/pallas_call | solution.py:697
  249.7 0.7 slice.9
  250.4 0.1 constant_dynamic-slice_fusion
  250.5 0.0 copy-done
  250.5 0.0 copy-done.1
  250.5 0.2 fusion.3
  250.7 0.2 fusion.1
  250.9 0.1 broadcast_in_dim.2
  250.9 0.1 reshape.27
  251.0 1.3 fusion.6
  (2 shorter events, 0.0 us)
Async XLA Ops:
  0.6 249.8 %copy-start = (s32[8]{0:T(128)S(1)}, s32[8]{0:T(128)}, u32[]{:S(2)}) copy-start(s32[8]{0:T(128)} %param.19) | copy-start | bytes 100
  0.7 249.8 %copy-start.1 = (f32[8]{0:T(128)S(1)}, f32[8]{0:T(128)}, u32[]{:S(2)}) copy-start(f32[8]{0:T(128)} %param.18) | copy-start | bytes 100

commit v5 on v4

--- a/solution.py
+++ b/solution.py
@@ -8,10 +8,14 @@
 RLEN = 64
 SIDE = 4
 BLOCK = 16
-ROWS = 32
+ROWS = 16
 HALF = ROWS // 2
 PER = ROWS // BLOCK
 CHUNK = 64
+PLAIN = 4
+BEHIND = 2
+FANOUT = 7
+DIRECT = 12
 LANES = 128
 
 epsilon = 1e-05
@@ -32,24 +36,23 @@
     row, column = section // SIDE, section % SIDE
     far = column if mirror else last - column
     step = 1 if mirror else -1
-
-    def any_of(spots):
-        flag = jnp.bool_(False)
-        for r, f in spots:
-            flag = jnp.logical_or(flag, jnp.logical_and(row == r, far == f))
-        return flag
-
-    along = jnp.logical_or(jnp.logical_and(row < last, far < last), any_of([(3, 0)]))
-    above = ((row + 1) % SIDE) * SIDE + column
-    below = ((row + SIDE - 1) % SIDE) * SIDE + column
-    edges = [
-        (along, section + step),
-        (any_of([(3, 0), (0, 0), (2, 2), (2, 3)]), above),
-        (any_of([(3, 0)]), below),
-    ]
-    start = jnp.where(row == 1, 2, 1)
-    depth = jnp.where(row == last, jnp.where(far < 2, far, far + 2), start + far)
-    return edges, depth
+    root_row = 0 if mirror else last
+    root = jnp.logical_and(far == 0, row == root_row)
+    starts = jnp.logical_and(far == 0, row < last)
+    chain = jnp.logical_and(far < last, row < last)
+    below = jnp.logical_and(far > 0, row == last - 1)
+    never = jnp.bool_(False)
+
+    def to_row(r):
+        return r * SIDE + column
+
+    edges = [(root, root, to_row(r)) for r in ((2, 1, 3) if mirror else (2, 0, 1))]
+    edges.append((below, below, to_row(last)))
+    edges += [(never, starts, section + step * d) for d in (3, 2)]
+    edges.append((chain, starts, section + step))
+    delay = jnp.where(row == root_row, 0, 1) + far
+    delay = delay + jnp.where(jnp.logical_and(far > 0, row == last), 1 if mirror else 2, 0)
+    return edges, delay + (1 if mirror else 0)
 
 
 def kernel(
@@ -76,19 +79,22 @@
     group = lax.axis_index("group")
     core = tensor % 2
     twin = tensor + 1 - 2 * core
-    first_section = section == 0
+    plain = section < PLAIN
+    next_plain = section + 1 < PLAIN
     last_section = section == section_count - 1
+    next_ahead = jnp.logical_not(jnp.logical_or(next_plain, last_section))
+    closes = jnp.logical_or(next_plain, last_section)
     in_first = group == 0
     in_second = group == 1
     late_half = section >= section_count // 2
-    entry = SIDE * (SIDE - 1)
-    edges_a, depth_a = tree_edges(section, False)
-    edges_b, depth_b = tree_edges(section, True)
-    lag = depth_b + 1 - depth_a
+    edges_a, delay_a = tree_edges(section, False)
+    edges_b, delay_b = tree_edges(section, True)
+    lag = (delay_b - delay_a) * 3 // 2
     lag_a = jnp.where(in_first, jnp.maximum(-lag, 0), 0)
     lag_b = jnp.where(in_first, jnp.maximum(lag, 0), 0)
     lag_most = jnp.maximum(lag_a, lag_b)
-    lag_limit = 6
+    lag_limit = 9
+    entry = 0
     crossing_out = jnp.logical_and(last_section, in_second)
     policy_source = jnp.logical_and(in_first, late_half)
     policy_passes = jnp.logical_and(in_second, late_half)
@@ -111,7 +117,7 @@
 
     places = batches * PER
 
-    @pl.when(section < 2)
+    @pl.when(section == 0)
     def _():
         def fetch(place, carry):
             own_block(x_ref, stream, place, stream_recv).start()
@@ -153,7 +159,7 @@
     def _():
         greet({"section": across})
 
-    @pl.when(jnp.logical_and(in_second, jnp.logical_not(first_section)))
+    @pl.when(jnp.logical_and(in_second, section > 0))
     def _():
         greet({"section": section - 1})
 
@@ -161,7 +167,7 @@
     def _():
         greet({"section": section + 1})
 
-    @pl.when(jnp.logical_not(first_section))
+    @pl.when(section > 0)
     def _():
         greet({"section": section - 1, "tensor": twin})
 
@@ -169,7 +175,7 @@
     def _():
         greet({"section": section + 1, "tensor": twin})
 
-    neighbours = as_count(jnp.logical_not(first_section)) + as_count(jnp.logical_not(last_section))
+    neighbours = as_count(section > 0) + as_count(jnp.logical_not(last_section))
     pl.semaphore_wait(
         barrier,
         tensor_count - 1 + section_count + neighbours + jnp.where(in_first, section_count - 1, neighbours + 1),
@@ -197,7 +203,7 @@
         device_id_type=MESH,
     )
 
-    @pl.when(jnp.logical_not(last_section))
+    @pl.when(next_ahead)
     def _():
         weight_copy.start()
 
@@ -238,9 +244,9 @@
             device_id_type=MESH,
         )
 
-    def stream_copy(batch):
+    def stream_copy(batch, source):
         return pltpu.make_async_remote_copy(
-            src_ref=leaving.at[batch],
+            src_ref=source.at[batch],
             dst_ref=stream.at[batch],
             send_sem=stream_send.at[batch],
             recv_sem=stream_recv.at[batch],
@@ -261,17 +267,22 @@
     def crossing_copy(batch):
         return final_copy(ending.at[batch], batches + batch, 0, {"section": entry, "group": 0})
 
+    def sends_now(edge, batch):
+        return jnp.logical_or(
+            jnp.logical_and(batch < DIRECT, edge[0]), jnp.logical_and(batch >= DIRECT, edge[1])
+        )
+
     def set_up():
         loads[0].wait()
         loads[1].wait()
 
-        @pl.when(first_section)
+        @pl.when(plain)
         def _():
             before_ref[...] = jnp.zeros_like(before_ref)
             blend[...] = jnp.zeros_like(blend)
             arrived[...] = jnp.zeros_like(arrived)
 
-        @pl.when(jnp.logical_not(first_section))
+        @pl.when(jnp.logical_not(plain))
         def _():
             all_bytes(before_ref, weight_recv).wait()
             share = units // tensor_count
@@ -315,19 +326,19 @@
             ).start()
 
     def stage_c(batch):
-        @pl.when(jnp.logical_not(first_section))
+        @pl.when(jnp.logical_not(plain))
         def _():
             for half in range(2):
                 all_bytes(arrived.at[batch, half], unit_recv.at[batch, half]).wait()
 
-        hidden = jnp.concatenate([arrived[batch, 0], arrived[batch, 1]], 0)
+        hidden = jnp.concatenate([arrived[batch, 0], arrived[batch, 1]], 0).astype(jnp.bfloat16)
         update = jnp.dot(hidden, before_ref[...], preferred_element_type=jnp.float32)
         fresh = (stream[batch].astype(jnp.float32) + update).astype(jnp.bfloat16)
         leaving[batch] = fresh
 
-        @pl.when(jnp.logical_and(section > 0, jnp.logical_not(last_section)))
-        def _():
-            stream_copy(batch).start()
+        @pl.when(next_ahead)
+        def _():
+            stream_copy(batch, leaving).start()
 
         values = fresh.astype(jnp.float32)
         squares = jnp.broadcast_to(jnp.sum(values * values, axis=1, keepdims=True), (ROWS, LANES))
@@ -339,12 +350,12 @@
             ).start()
 
     def stage_b(batch):
-        @pl.when(jnp.logical_and(batch == 0, jnp.logical_not(first_section)))
+        @pl.when(jnp.logical_and(batch == 0, jnp.logical_not(plain)))
         def _():
             all_bytes(blend.at[pl.ds(0, tensor_count - 1)], blend_recv.at[1]).wait()
 
         ahead = jnp.dot(
-            arrived[batch, core],
+            arrived[batch, core].astype(jnp.bfloat16),
             blend[...].reshape(units, 2 * units),
             preferred_element_type=jnp.float32,
         )
@@ -359,14 +370,14 @@
         scale = lax.rsqrt(squares[:, :1] / (width * tensor_count) + epsilon)
         gate = (total[:HALF] + ahead[:, :units]) * scale
         up = (total[HALF:] + ahead[:, units:]) * scale
-        mine[batch] = (gate / (1.0 + jnp.exp(-gate)) * up).astype(jnp.bfloat16)
-
-        @pl.when(jnp.logical_not(last_section))
+        mine[batch] = gate / (1.0 + jnp.exp(-gate)) * up
+
+        @pl.when(next_ahead)
         def _():
             unit_copy(batch, tensor).start()
             unit_copy(batch, twin).start()
 
-        @pl.when(last_section)
+        @pl.when(closes)
         def _():
             twin_copy(batch).start()
 
@@ -375,17 +386,23 @@
         here, there = mine[batch], twin_rows[batch]
         hidden = jnp.concatenate(
             [jnp.where(core == 0, here, there), jnp.where(core == 0, there, here)], 0
-        )
+        ).astype(jnp.bfloat16)
         update = jnp.dot(hidden, wout_ref[...], preferred_element_type=jnp.float32)
         ending[batch] = (leaving[batch].astype(jnp.float32) + update).astype(jnp.bfloat16)
 
-        @pl.when(in_first)
+        @pl.when(next_plain)
+        def _():
+            stream_copy(batch, ending).start()
+
+        @pl.when(jnp.logical_and(last_section, in_first))
         def _():
             final[batch] = ending[batch]
-            for edge, (_, target) in enumerate(edges_a):
-                final_copy(ending.at[batch], batch, edge, {"section": target}).start()
-
-        @pl.when(in_second)
+            for edge, way in enumerate(edges_a):
+                @pl.when(sends_now(way, batch))
+                def _(edge=edge, target=way[2]):
+                    final_copy(ending.at[batch], batch, edge, {"section": target}).start()
+
+        @pl.when(crossing_out)
         def _():
             crossing_copy(batch).start()
 
@@ -397,32 +414,32 @@
             def _():
                 stage_a(index)
 
-            @pl.when(index >= 1)
-            def _():
-                stage_b(index - 1)
+            @pl.when(index >= BEHIND)
+            def _():
+                stage_b(index - BEHIND)
 
             @pl.when(index < batches)
             def _():
                 stage_c(index)
 
-            @pl.when(jnp.logical_and(index >= 1, last_section))
-            def _():
-                stage_d(index - 1)
+            @pl.when(jnp.logical_and(index >= BEHIND, closes))
+            def _():
+                stage_d(index - BEHIND)
 
             return carry
 
-        lax.fori_loop(0, batches + 1, step, 0)
-
-    def pass_on(slot, edges, root):
+        lax.fori_loop(0, batches + BEHIND, step, 0)
+
+    def pass_on(batch, slot, edges, root):
         @pl.when(jnp.logical_not(root))
         def _():
             all_bytes(final.at[slot], final_recv.at[slot]).wait()
 
             @pl.when(in_first)
             def _():
-                for edge, (sends, target) in enumerate(edges):
-                    @pl.when(sends)
-                    def _(edge=edge, target=target):
+                for edge, way in enumerate(edges):
+                    @pl.when(sends_now(way, batch))
+                    def _(edge=edge, target=way[2]):
                         final_copy(final.at[slot], slot, edge, {"section": target}).start()
 
             @pl.when(jnp.logical_and(policy_passes, slot < batches))
@@ -520,11 +537,11 @@
         def step(index, carry):
             @pl.when(jnp.logical_and(index >= lag_a, index < batches + lag_a))
             def _():
-                pass_on(index - lag_a, edges_a, jnp.logical_and(last_section, in_first))
+                pass_on(index - lag_a, index - lag_a, edges_a, jnp.logical_and(last_section, in_first))
 
             @pl.when(jnp.logical_and(index >= lag_b, index < batches + lag_b))
             def _():
-                pass_on(batches + index - lag_b, edges_b, jnp.bool_(False))
+                pass_on(index - lag_b, batches + index - lag_b, edges_b, jnp.bool_(False))
 
             done = index - lag_most + 1
             chunk = done // per_chunk - 1
@@ -587,24 +604,24 @@
         all_bytes(pieces.at[batch], piece_send.at[batch]).wait()
         all_bytes(square_in.at[batch], square_send.at[batch]).wait()
 
+        @pl.when(next_ahead)
+        def _():
+            all_bytes(arrived.at[batch], unit_send.at[batch]).wait()
+
+        @pl.when(closes)
+        def _():
+            twin_copy(batch).wait_send()
+
         @pl.when(jnp.logical_not(last_section))
         def _():
-            all_bytes(arrived.at[batch], unit_send.at[batch]).wait()
-
-        @pl.when(last_section)
-        def _():
-            twin_copy(batch).wait_send()
-
-        @pl.when(jnp.logical_and(section > 0, jnp.logical_not(last_section)))
-        def _():
-            stream_copy(batch).wait_send()
+            stream_copy(batch, leaving).wait_send()
 
         @pl.when(in_first)
         def _():
             for first, edges in ((0, edges_a), (batches, edges_b)):
-                for edge, (sends, target) in enumerate(edges):
-                    @pl.when(sends)
-                    def _(edge=edge, target=target, slot=first + batch):
+                for edge, way in enumerate(edges):
+                    @pl.when(sends_now(way, batch))
+                    def _(edge=edge, target=way[2], slot=first + batch):
                         final_copy(final.at[slot], slot, edge, {"section": target}).wait_send()
 
         @pl.when(policy_source)
@@ -622,11 +639,11 @@
 
         return carry
 
-    @pl.when(jnp.logical_not(last_section))
+    @pl.when(next_ahead)
     def _():
         weight_copy.wait_send()
 
-    @pl.when(jnp.logical_not(first_section))
+    @pl.when(jnp.logical_not(plain))
     def _():
         for index in range(2):
             all_bytes(blend_in, blend_send.at[index]).wait()
@@ -714,9 +731,9 @@
             pltpu.VMEM((batches, tensor_count - 1, ROWS, units), bf16),
             pltpu.VMEM((batches, 2, HALF, LANES), f32),
             pltpu.VMEM((batches, tensor_count - 1, HALF, LANES), f32),
-            pltpu.VMEM((batches, HALF, units), bf16),
-            pltpu.VMEM((batches, 2, HALF, units), bf16),
-            pltpu.VMEM((batches, HALF, units), bf16),
+            pltpu.VMEM((batches, HALF, units), f32),
+            pltpu.VMEM((batches, 2, HALF, units), f32),
+            pltpu.VMEM((batches, HALF, units), f32),
             pltpu.VMEM((batches, ROWS, width), bf16),
             pltpu.VMEM((batches, ROWS, width), bf16),
             pltpu.VMEM((2 * batches, ROWS, width), bf16),
@@ -742,7 +759,7 @@
             dma((batches,)),
             dma((batches,)),
             dma((batches,)),
-            dma((2 * batches, 3)),
+            dma((2 * batches, FANOUT)),
             dma((2 * batches,)),
             dma((blocks,)),
             dma((chunks,)),

time: 252 us -> 234 us (0.929)
  Pallas kernels: 249 us -> 230 us
    pallas_call x1, Pallas kernels: 249 us -> 230 us  [token_terms(): pl.pallas_call(kernel, out_shape=jax.ShapeDtypeStruct((8, LANES), f32), i...]
where the time goes in v5:
time: 234 us; the launch traced here: 233 us
  Pallas kernels  230 us (98%)
    pallas_call x1, Pallas kernels, token_terms(): pl.pallas_call(kernel, out_shape=jax.ShapeDtypeStruct((8, LANES), f32), i...  230 us

profile of v5, /device:TPU:1, one launch (start us, length us, event | category | flops | bytes accessed | tf_op | source)
XLA Modules:
  0.0 233.5 jit_solution(17962439553684879722)
XLA Ops:
  0.6 0.0 copy-start
  0.7 0.0 copy-start.1
  0.7 230.2 %token_terms.1 = f32[8,128]{1,0:T(8,128)} custom-call(bf16[16,16,2048]{2,1,0:T(8,128)(2,1)} %bitcast.20, f32[1,2048]{1,0:T(1,128)} %gain_hbm.1, bf16[2048,768]{1,0:T(8,128)(2,1)} %bitcast.18, bf16[384,2048]{1,0:T(8,128)(2,1)} %bitcast.19, bf16[16,16,2048]{2,1,0:T(8,128)(2,1)} %bitcast.21, bf16[1024,2048]{1,0:T(8,128)(2,1)} %bitcast.17, s32[4,128]{1,0:T(4,128)} %bitcast.22), custom_call_target="tpu_custom_call" | custom-call | tf_op jit(solution)/shard_map/token_terms/pallas_call | solution.py:714
  230.8 0.7 slice.9
  231.5 0.1 constant_dynamic-slice_fusion
  231.6 0.0 copy-done
  231.6 0.0 copy-done.1
  231.6 0.2 fusion.3
  231.8 0.2 fusion.1
  232.0 0.1 broadcast_in_dim.2
  232.1 0.1 reshape.27
  232.2 1.3 fusion.6
  (2 shorter events, 0.0 us)
Async XLA Ops:
  0.6 231.0 %copy-start = (s32[8]{0:T(128)S(1)}, s32[8]{0:T(128)}, u32[]{:S(2)}) copy-start(s32[8]{0:T(128)} %param.19) | copy-start | bytes 100
  0.7 231.0 %copy-start.1 = (f32[8]{0:T(128)S(1)}, f32[8]{0:T(128)}, u32[]{:S(2)}) copy-start(f32[8]{0:T(128)} %param.18) | copy-start | bytes 100

commit v6 on v5

--- a/solution.py
+++ b/solution.py
@@ -12,10 +12,10 @@
 HALF = ROWS // 2
 PER = ROWS // BLOCK
 CHUNK = 64
-PLAIN = 4
+PLAIN = 6
 BEHIND = 2
 FANOUT = 7
-DIRECT = 12
+DIRECT = 14
 LANES = 128
 
 epsilon = 1e-05
@@ -36,23 +36,27 @@
     row, column = section // SIDE, section % SIDE
     far = column if mirror else last - column
     step = 1 if mirror else -1
-    root_row = 0 if mirror else last
-    root = jnp.logical_and(far == 0, row == root_row)
+    source = jnp.logical_and(far == 0, row == last)
     starts = jnp.logical_and(far == 0, row < last)
     chain = jnp.logical_and(far < last, row < last)
-    below = jnp.logical_and(far > 0, row == last - 1)
     never = jnp.bool_(False)
 
     def to_row(r):
-        return r * SIDE + column
-
-    edges = [(root, root, to_row(r)) for r in ((2, 1, 3) if mirror else (2, 0, 1))]
-    edges.append((below, below, to_row(last)))
+        return (r % SIDE) * SIDE + column
+
+    down = jnp.logical_and(far == 0, row < last - 1)
+    edges = [(down, down, to_row(row + 1))]
+    if mirror:
+        ends = row == last - 1
+        edges.append((ends, ends, to_row(last)))
+        delay = row + 1 + far
+    else:
+        ends = jnp.logical_and(row == 0, far > 0)
+        edges += [(ends, ends, to_row(last)), (source, source, to_row(0))]
+        delay = jnp.where(row == last, jnp.where(far == 0, 0, 2 + far), row + 1 + far)
     edges += [(never, starts, section + step * d) for d in (3, 2)]
     edges.append((chain, starts, section + step))
-    delay = jnp.where(row == root_row, 0, 1) + far
-    delay = delay + jnp.where(jnp.logical_and(far > 0, row == last), 1 if mirror else 2, 0)
-    return edges, delay + (1 if mirror else 0)
+    return edges, delay
 
 
 def kernel(
@@ -93,7 +97,7 @@
     lag_a = jnp.where(in_first, jnp.maximum(-lag, 0), 0)
     lag_b = jnp.where(in_first, jnp.maximum(lag, 0), 0)
     lag_most = jnp.maximum(lag_a, lag_b)
-    lag_limit = 9
+    lag_limit = 10
     entry = 0
     crossing_out = jnp.logical_and(last_section, in_second)
     policy_source = jnp.logical_and(in_first, late_half)
@@ -125,8 +129,8 @@
 
         lax.fori_loop(0, places, fetch, 0)
 
-    for load in loads:
-        load.start()
+    for index in (2, 0, 1, 3, 4):
+        loads[index].start()
 
     @pl.when(in_second)
     def _():
@@ -194,18 +198,25 @@
             device_id_type=MESH,
         )
 
-    weight_copy = pltpu.make_async_remote_copy(
-        src_ref=wout_hbm,
-        dst_ref=before_ref,
-        send_sem=weight_send,
-        recv_sem=weight_recv,
-        device_id={"section": section + 1},
-        device_id_type=MESH,
-    )
+    share = units // tensor_count
+
+    def weight_copy(pair):
+        rows = pl.ds(pl.multiple_of(pair * 2 * share, 2 * share), 2 * share)
+        return pltpu.make_async_remote_copy(
+            src_ref=wout_ref.at[rows],
+            dst_ref=before_ref.at[rows],
+            send_sem=weight_send.at[pair],
+            recv_sem=weight_recv.at[pair],
+            device_id={"section": section + 1},
+            device_id_type=MESH,
+        )
+
+    loads[2].wait()
 
     @pl.when(next_ahead)
     def _():
-        weight_copy.start()
+        for pair in range(tensor_count // 2):
+            weight_copy(pair).start()
 
     def policy_copy(place):
         return pltpu.make_async_remote_copy(
@@ -284,22 +295,26 @@
 
         @pl.when(jnp.logical_not(plain))
         def _():
-            all_bytes(before_ref, weight_recv).wait()
-            share = units // tensor_count
-
             def product(pair, carry):
+                weight_copy(pair).wait_recv()
                 rows = pl.ds(pl.multiple_of(pair * 2 * share, 2 * share), 2 * share)
                 scaled = (before_ref[rows].astype(jnp.float32) * gain_ref[...]).astype(jnp.bfloat16)
                 out = jnp.dot(scaled, win_ref[...], preferred_element_type=jnp.float32)
                 blend_out[pl.ds(pair * 2, 2)] = out.astype(jnp.bfloat16).reshape(2, share, 2 * units)
+                for side in range(2):
+                    target = pair * 2 + side
+                    offset = (target + tensor_count - tensor) % tensor_count
+
+                    @pl.when(offset > 0)
+                    def _(target=target, offset=offset):
+                        to_peer(
+                            blend_out.at[target], blend_in.at[offset - 1],
+                            blend_send.at[0], blend_recv.at[0], offset,
+                        ).start()
+
                 return carry
 
             lax.fori_loop(0, tensor_count // 2, product, 0)
-            for offset in range(1, tensor_count):
-                to_peer(
-                    blend_out.at[(tensor + offset) % tensor_count], blend_in.at[offset - 1],
-                    blend_send.at[0], blend_recv.at[0], offset,
-                ).start()
             all_bytes(blend_in, blend_recv.at[0]).wait()
             total = blend_out[tensor].astype(jnp.float32)
             for offset in range(1, tensor_count):
@@ -407,8 +422,6 @@
             crossing_copy(batch).start()
 
     def relay():
-        loads[2].wait()
-
         def step(index, carry):
             @pl.when(index < batches)
             def _():
@@ -641,7 +654,8 @@
 
     @pl.when(next_ahead)
     def _():
-        weight_copy.wait_send()
+        for pair in range(tensor_count // 2):
+            weight_copy(pair).wait_send()
 
     @pl.when(jnp.logical_not(plain))
     def _():
@@ -745,8 +759,8 @@
             pltpu.VMEM((8, LANES), f32),
             pltpu.VMEM((2 * section_count, 8, LANES), f32),
             dma((5,)),
-            dma,
-            dma,
+            dma((tensor_count // 2,)),
+            dma((tensor_count // 2,)),
             dma((2,)),
             dma((2,)),
             dma((batches,)),

time: 234 us -> 226 us (0.966)
  Pallas kernels: 230 us -> 222 us
    pallas_call x1, Pallas kernels: 230 us -> 222 us  [token_terms(): pl.pallas_call(kernel, out_shape=jax.ShapeDtypeStruct((8, LANES), f32), i...]
where the time goes in v6:
time: 226 us; the launch traced here: 225 us
  Pallas kernels  222 us (98%)
    pallas_call x1, Pallas kernels, token_terms(): pl.pallas_call(kernel, out_shape=jax.ShapeDtypeStruct((8, LANES), f32), i...  222 us

profile of v6, /device:TPU:1, one launch (start us, length us, event | category | flops | bytes accessed | tf_op | source)
XLA Modules:
  0.0 225.4 jit_solution(18247679193565681356)
XLA Ops:
  0.6 0.0 copy-start
  0.7 0.0 copy-start.1
  0.7 222.2 %token_terms.1 = f32[8,128]{1,0:T(8,128)} custom-call(bf16[16,16,2048]{2,1,0:T(8,128)(2,1)} %bitcast.20, f32[1,2048]{1,0:T(1,128)} %gain_hbm.1, bf16[2048,768]{1,0:T(8,128)(2,1)} %bitcast.18, bf16[384,2048]{1,0:T(8,128)(2,1)} %bitcast.19, bf16[16,16,2048]{2,1,0:T(8,128)(2,1)} %bitcast.21, bf16[1024,2048]{1,0:T(8,128)(2,1)} %bitcast.17, s32[4,128]{1,0:T(4,128)} %bitcast.22), custom_call_target="tpu_custom_call" | custom-call | tf_op jit(solution)/shard_map/token_terms/pallas_call | solution.py:728
  222.8 0.7 slice.9
  223.5 0.1 constant_dynamic-slice_fusion
  223.6 0.0 copy-done
  223.6 0.0 copy-done.1
  223.6 0.2 fusion.3
  223.8 0.2 fusion.1
  224.0 0.1 broadcast_in_dim.2
  224.1 0.1 reshape.27
  224.2 1.3 fusion.6
  (2 shorter events, 0.0 us)
Async XLA Ops:
  0.6 223.0 %copy-start = (s32[8]{0:T(128)S(1)}, s32[8]{0:T(128)}, u32[]{:S(2)}) copy-start(s32[8]{0:T(128)} %param.19) | copy-start | bytes 100
  0.7 223.0 %copy-start.1 = (f32[8]{0:T(128)S(1)}, f32[8]{0:T(128)}, u32[]{:S(2)}) copy-start(f32[8]{0:T(128)} %param.18) | copy-start | bytes 100
